TPU v7x, 128 devices: a whole 4x4x4 slice. The times are simulated.
128 devices in a mesh: pipe: 2 (over core), exp: 8 (over z_hi, y), etp: 8 (over z_lo, x).
Axes of the slice: x: 4, y: 4, z: 4 (z_hi: 2, z_lo: 2; z = z_hi * 2 + z_lo), core: 2. Of those that a mesh axis runs over, the one named last changes fastest.
Arguments:
- inputs: bfloat16 [2, 2048, 3072], P('pipe', 'exp', 'etp'), may hold values from -6 to 6
- attn_gain: bfloat16 [2, 3072], P('pipe'), may hold values from 0.099609375 to 1.8984375
- query_weight: bfloat16 [2, 3072, 3072], P('pipe', None, 'etp'), may hold values from -2 to 2
- key_weight: bfloat16 [2, 3072, 1024], P('pipe', None, 'etp'), may hold values from -2 to 2
- value_weight: bfloat16 [2, 3072, 1024], P('pipe', None, 'etp'), may hold values from -0.109375 to 0.109375
- out_weight: bfloat16 [2, 3072, 3072], P('pipe', 'etp'), may hold values from -0.109375 to 0.109375
- ffn_gain: bfloat16 [2, 3072], P('pipe'), may hold values from 0.099609375 to 1.8984375
- gate_weight: bfloat16 [2, 8, 3072, 8192], P('pipe', 'exp', None, 'etp'), may hold values from -0.109375 to 0.109375
- up_weight: bfloat16 [2, 8, 3072, 8192], P('pipe', 'exp', None, 'etp'), may hold values from -0.109375 to 0.109375
- down_weight: bfloat16 [2, 8, 8192, 3072], P('pipe', 'exp', 'etp'), may hold values from -0.0625 to 0.0625
- expert_ids: int32 [2, 2048, 2], P('pipe', ('exp', 'etp')), may hold values from 0 to 7, all different within a row; in each aligned block of 32 rows (0 to 31, 32 to 63, ..., all dimensions but the last counted through in order) at most 16 rows name the same one
- route_weights: float32 [2, 2048, 2], P('pipe', ('exp', 'etp')), may hold values from 0.2 to 1
Outputs:
- handed: bfloat16 [2, 2048, 3072], P('pipe', ('exp', 'etp'))
Inputs may be any that keep to these rules, and one draw needn't show every extreme that they name: `expert_ids`: within the 32 tokens of one device, no expert is named by more than 16 routes, a bound that some block reaches; a token's two experts differ.
All inputs are finite; a program needn't handle non-finite values.
Results may differ from a plain program's by a relative error of at most 0.022.
Values may be sent and summed in bfloat16 or wider, within the bound.
A program may use at most 128 MiB of HBM per device.

v0:
```python
import jax
import jax.numpy as jnp
from jax import lax
from jax.sharding import PartitionSpec as P

HQ = 24
HK = 8
HD = 128
CAP = 16


epsilon = 1e-05
rope_base = 1000000.0


def from_behind(block, axis, distance):
    devices = range(lax.axis_size(axis))
    route = [((i - distance) % len(devices), i) for i in devices]
    return lax.ppermute(block, axis, route)


def rms_scale(values_in, gain):
    floats = values_in.astype(jnp.float32)
    factor = lax.rsqrt(jnp.mean(floats * floats, axis=-1, keepdims=True) + epsilon)
    return (floats * factor * gain.astype(jnp.float32)).astype(jnp.bfloat16)


def rotate(tensor):
    seq_len = tensor.shape[0]
    half_dim = tensor.shape[2] // 2
    freqs = rope_base ** (-jnp.arange(half_dim, dtype=jnp.float32) / half_dim)
    angles = jnp.arange(seq_len, dtype=jnp.float32)[:, None] * freqs[None, :]
    cosine = jnp.cos(angles)[:, None, :]
    sine = jnp.sin(angles)[:, None, :]
    first = tensor[..., :half_dim]
    second = tensor[..., half_dim:]
    return jnp.concatenate(
        [first * cosine - second * sine, second * cosine + first * sine], axis=-1
    )


def attend(normed, query_w, key_w, value_w, heads_q, heads_k):
    seq_len = normed.shape[0]
    queries = rotate(
        jnp.dot(normed, query_w, preferred_element_type=jnp.float32).reshape(seq_len, heads_q, HD)
    ).astype(jnp.bfloat16)
    keys_rot = rotate(
        jnp.dot(normed, key_w, preferred_element_type=jnp.float32).reshape(seq_len, heads_k, HD)
    ).astype(jnp.bfloat16)
    values = (
        jnp.dot(normed, value_w, preferred_element_type=jnp.float32)
        .astype(jnp.bfloat16)
        .reshape(seq_len, heads_k, HD)
    )
    group_ratio = heads_q // heads_k
    grouped = queries.reshape(seq_len, heads_k, group_ratio, HD)
    scores = jnp.einsum(
        "skrd,tkd->krst", grouped, keys_rot, preferred_element_type=jnp.float32
    ) * HD ** (-0.5)
    causal = jnp.arange(seq_len)[:, None] >= jnp.arange(seq_len)[None, :]
    scores = jnp.where(causal, scores, -1e30)
    peak = jnp.max(scores, axis=-1, keepdims=True)
    expo = jnp.exp(scores - peak)
    weights_bf = (expo / jnp.sum(expo, axis=-1, keepdims=True)).astype(jnp.bfloat16)
    mixed = jnp.einsum(
        "krst,tkd->skrd", weights_bf, values, preferred_element_type=jnp.float32
    ).astype(jnp.bfloat16)
    return mixed.reshape(seq_len, heads_q * HD)


def placement(route_ids, experts):
    token_count = route_ids.shape[0]
    flat_ids = route_ids.reshape(-1)
    onehot = (flat_ids[:, None] == jnp.arange(experts, dtype=jnp.int32)[None, :]).astype(jnp.int32)
    before = jnp.cumsum(onehot, axis=0) - onehot
    slot_of = jnp.sum(onehot * before, axis=1)
    target = flat_ids * CAP + slot_of
    placed = (target[:, None] == jnp.arange(experts * CAP, dtype=jnp.int32)[None, :]).astype(
        jnp.float32
    )
    return placed.reshape(token_count, 2, experts * CAP)


def dispatch_table(route_ids, experts):
    return jnp.sum(placement(route_ids, experts), axis=1).T.astype(jnp.bfloat16)


def expert_hidden(routed_rows, gate_w, up_w):
    gate = jnp.dot(routed_rows, gate_w, preferred_element_type=jnp.float32)
    upper = jnp.dot(routed_rows, up_w, preferred_element_type=jnp.float32)
    return (jax.nn.silu(gate) * upper).astype(jnp.bfloat16)


def on_device(
    inputs,
    attn_gain,
    query_weight,
    key_weight,
    value_weight,
    out_weight,
    ffn_gain,
    gate_weight,
    up_weight,
    down_weight,
    expert_ids,
    route_weights,
):
    tp_count = lax.axis_size("etp")
    ep_count = lax.axis_size("exp")
    tp_index = lax.axis_index("etp")
    token_count = expert_ids.shape[1]
    width = attn_gain.shape[1]
    gate_w = gate_weight[0, 0]
    up_w = up_weight[0, 0]
    down_w = down_weight[0, 0]
    sequence = lax.all_gather(inputs[0], "etp", axis=1, tiled=True)
    normed = rms_scale(sequence, attn_gain[0])
    heads_q = HQ // tp_count
    heads_k = HK // tp_count
    mixed = attend(normed, query_weight[0], key_weight[0], value_weight[0], heads_q, heads_k)
    summed = lax.psum(
        jnp.dot(mixed, out_weight[0], preferred_element_type=jnp.float32).astype(jnp.bfloat16),
        "etp",
    ).astype(jnp.float32)
    state_all = (sequence.astype(jnp.float32) + summed).astype(jnp.bfloat16)
    state = lax.dynamic_slice_in_dim(state_all, tp_index * token_count, token_count, 0)
    ffn_all = rms_scale(state_all, ffn_gain[0])
    ids_all = lax.all_gather(expert_ids[0], "etp", axis=0, tiled=True)
    tables = jax.vmap(lambda block_ids: dispatch_table(block_ids, ep_count))(
        ids_all.reshape(tp_count, token_count, 2)
    )
    outgoing = jnp.einsum(
        "bst,btd->bsd",
        tables,
        ffn_all.reshape(tp_count, token_count, width),
        preferred_element_type=jnp.float32,
    ).astype(jnp.bfloat16)
    outgoing = outgoing.reshape(tp_count, ep_count, CAP, width)
    received = lax.all_to_all(outgoing, "exp", split_axis=1, concat_axis=1, tiled=True)
    hidden = expert_hidden(received.reshape(-1, width), gate_w, up_w)
    expert_out = lax.psum_scatter(
        jnp.dot(hidden, down_w, preferred_element_type=jnp.float32).astype(jnp.bfloat16),
        "etp",
        scatter_dimension=0,
        tiled=True,
    )
    returned = lax.all_to_all(
        expert_out.reshape(ep_count, CAP, width), "exp", split_axis=0, concat_axis=0, tiled=True
    )
    placed = placement(expert_ids[0], ep_count)
    combine = jnp.sum(placed * route_weights[0][:, :, None], axis=1)
    moe_part = jnp.dot(
        combine, returned.reshape(-1, width).astype(jnp.float32), precision=lax.Precision.HIGHEST
    )
    layer_out = (state.astype(jnp.float32) + moe_part).astype(jnp.bfloat16)
    handed = from_behind(layer_out, "pipe", 1)
    return handed[None]


def solution(mesh):
    in_specs = (
        P("pipe", "exp", "etp"),
        P("pipe", None),
        P("pipe", None, "etp"),
        P("pipe", None, "etp"),
        P("pipe", None, "etp"),
        P("pipe", "etp", None),
        P("pipe", None),
        P("pipe", "exp", None, "etp"),
        P("pipe", "exp", None, "etp"),
        P("pipe", "exp", "etp", None),
        P("pipe", ("exp", "etp"), None),
        P("pipe", ("exp", "etp"), None),
    )
    out_specs = P("pipe", ("exp", "etp"), None)
    return jax.shard_map(
        on_device, mesh=mesh, in_specs=in_specs, out_specs=out_specs, check_vma=False
    )
```

profile of v0, /device:TPU:1, one launch (start us, length us, event | category | flops | bytes accessed | tf_op | source)
XLA Modules:
  0.0 360.4 jit_solution(7419827755595464241)
XLA Ops:
  8.0 4.3 %copy.91 = bf16[1,3072,384]{1,2,0:T(8,128)(2,1)} copy(bf16[1,3072,384]{2,1,0:T(8,128)(2,1)} %param.14) | data formatting | bytes 4718592 | tf_op args[2]
  12.7 33.8 %all-gather.4.cloned.1.call-done = bf16[1,256,3072]{2,1,0:T(8,128)(2,1)} async-done(((bf16[1,256,384]{2,1,0:T(8,128)(2,1)}), bf16[1,256,3072]{2,1,0:T(8,128)(2,1)}) %all-gather.4.cloned.1.call-update) | async-done | bytes 1572880 | tf_op jit(solution)/shard_map/all_gather | solution.py:116
  46.5 1.9 fusion.13
  48.4 2.4 convolution_bitcast_fusion
  51.2 0.9 fusion.22
  52.6 2.5 convolution_convert_fusion.2
  55.1 2.2 convolution_convert_fusion.1
  57.5 22.4 %all-gather.1 = s32[1,256,2]{2,0,1:T(1,128)S(1)} all-gather(s32[1,32,2]{2,0,1:T(1,128)S(1)} %copy.98), channel_id=3, replica_groups=mesh['pipe'=2,'exp'=8,'etp'=8] {'etp'}, dimensions={1}, use_global_device_ids=true | all-gather | bytes 2304 | tf_op jit(solution)/shard_map/all_gather | solution.py:128
  80.5 1.0 reduce.5
  81.7 1.4 fusion.58
  83.4 54.7 %all-reduce.2.cloned.1.call-done = bf16[256,3072]{1,0:T(8,128)(2,1)} async-done(((bf16[256,3072]{1,0:T(8,128)(2,1)}), bf16[256,3072]{1,0:T(8,128)(2,1)}) %all-reduce.2.cloned.1.call-update) | async-done | bytes 1572880 | tf_op jit(solution)/shard_map/psum | solution.py:121
  138.1 2.6 fusion.10
  141.3 1.8 convolution_convert_fusion
  143.1 0.8 copy.103
  143.9 74.1 %all_to_all.10 = bf16[8,8,16,3072]{3,2,0,1:T(8,128)(2,1)S(1)} all-to-all(bf16[8,8,16,3072]{3,2,0,1:T(8,128)(2,1)S(1)} %copy.103), channel_id=1, replica_groups=mesh['pipe'=2,'exp'=8,'etp'=8] {'exp'}, dimensions={1} | all-to-all | bytes 12582912 | tf_op jit(solution)/shard_map/all_to_all | solution.py:139
  218.8 2.7 copy-done.3
  221.5 10.1 %fusion.2 = f32[1024,1024]{1,0:T(8,128)} fusion(bf16[1024,3072]{1,0:T(8,128)(2,1)S(1)} %bitcast.99, bf16[1,1,3072,1024]{3,2,1,0:T(8,128)(2,1)} %param.20), kind=kOutput, calls=%fused_computation.2 | convolution fusion | flops 6442450944 | bytes 16777216 | tf_op jit(solution)/shard_map/dot_general | solution.py:90
  231.6 21.6 %fusion.6 = bf16[1024,3072]{1,0:T(8,128)(2,1)} fusion(bf16[1,1,1024,3072]{3,2,1,0:T(8,128)(2,1)} %param.21, f32[1024,1024]{1,0:T(8,128)} %fusion.2, bf16[1024,3072]{1,0:T(8,128)(2,1)} %bitcast.100, bf16[1,1,3072,1024]{3,2,1,0:T(8,128)(2,1)} %param.19), kind=kOutput, calls=%fused_computation.7 | convolution fusion | flops 12894339072 | bytes 29360128 | tf_op jit(solution)/shard_map/dot_general | solution.py:142
  253.2 75.8 %reduce-scatter.2.cloned.1.call-done = bf16[128,3072]{1,0:T(8,128)(2,1)} async-done(((bf16[1024,3072]{1,0:T(8,128)(2,1)}), bf16[128,3072]{1,0:T(8,128)(2,1)}) %reduce-scatter.2.cloned.1.call-update) | async-done | bytes 786448 | tf_op jit(solution)/shard_map/reduce_scatter | solution.py:141
  329.0 6.3 %all-to-all-start.1 = ((bf16[8,16,3072]{2,1,0:T(8,128)(2,1)}), bf16[8,16,3072]{2,1,0:T(8,128)(2,1)S(1)}, u32[]{:S(2)}, u32[]{:S(2)}) async-start(bf16[8,16,3072]{2,1,0:T(8,128)(2,1)} %bitcast.104), calls=%async_computation.2 | async-start | bytes 1572864 | tf_op jit(solution)/shard_map/all_to_all | solution.py:147
  336.2 13.7 %all-to-all-done.1 = bf16[8,16,3072]{2,1,0:T(8,128)(2,1)S(1)} async-done(((bf16[8,16,3072]{2,1,0:T(8,128)(2,1)}), bf16[8,16,3072]{2,1,0:T(8,128)(2,1)S(1)}, u32[]{:S(2)}, u32[]{:S(2)}) %all-to-all-start.1) | async-done | bytes 786464 | tf_op jit(solution)/shard_map/all_to_all | solution.py:147
  349.8 1.4 fusion.9
  351.2 0.9 collective-permute-start
  352.1 1.1 collective-permute-done
  (57 shorter events, 6.8 us)
Async XLA Ops:
  6.5 48.6 %copy-start = (bf16[1,384,3072]{2,1,0:T(8,128)(2,1)S(1)}, bf16[1,384,3072]{2,1,0:T(8,128)(2,1)}, u32[]{:S(2)}) copy-start(bf16[1,384,3072]{2,1,0:T(8,128)(2,1)} %param.17) | copy-start | bytes 7077892
  6.5 39.9 %all-gather.4.cloned.1.call-start = ((), (), s32[]{:S(2)}) async-start(), calls=%async_computation.5 | async-start | bytes 1769472 | tf_op jit(solution)/shard_map/all_gather | solution.py:116
  7.3 130.9 %all-reduce.2.cloned.1.call-start = ((), (), s32[]{:S(2)}) async-start(), calls=%async_computation.3 | async-start | bytes 3145728 | tf_op jit(solution)/shard_map/psum | solution.py:121
  46.5 4.7 %copy-start.4 = (bf16[1,256,3072]{2,1,0:T(8,128)(2,1)S(1)}, bf16[1,256,3072]{2,1,0:T(8,128)(2,1)}, u32[]{:S(2)}) copy-start(bf16[1,256,3072]{2,1,0:T(8,128)(2,1)} %all-gather.4.cloned.1.call-done) | copy-start | bytes 4718596
  46.5 4.7 %copy-start.5 = (bf16[1,3072,384]{1,2,0:T(8,128)(2,1)S(1)}, bf16[1,3072,384]{1,2,0:T(8,128)(2,1)}, u32[]{:S(2)}) copy-start(bf16[1,3072,384]{1,2,0:T(8,128)(2,1)} %copy.91) | copy-start | bytes 7077892
  55.1 2.3 copy-start.6
  55.1 2.3 copy-start.7
  57.3 271.7 %reduce-scatter.2.cloned.1.call-start = ((), (), s32[]{:S(2)}) async-start(), calls=%async_computation.4 | async-start | bytes 7077888 | tf_op jit(solution)/shard_map/reduce_scatter | solution.py:141
  140.8 2.4 copy-start.2
  218.8 2.7 copy-start.3
  253.2 82.9 %copy-start.8 = (f32[1,32,2]{1,2,0:T(2,128)S(1)}, f32[1,32,2]{1,2,0:T(2,128)}, u32[]{:S(2)}) copy-start(f32[1,32,2]{1,2,0:T(2,128)} %param.23) | copy-start | bytes 772
  253.2 100.6 %copy-start.1 = (bf16[1,384,3072]{2,1,0:T(8,128)(2,1)S(1)}, bf16[1,384,3072]{2,1,0:T(8,128)(2,1)}, u32[]{:S(2)}) copy-start(bf16[1,384,3072]{2,1,0:T(8,128)(2,1)} %param.17) | copy-start | bytes 7077892
  329.0 20.8 %all-to-all-start.1 = ((bf16[8,16,3072]{2,1,0:T(8,128)(2,1)}), bf16[8,16,3072]{2,1,0:T(8,128)(2,1)S(1)}, u32[]{:S(2)}, u32[]{:S(2)}) async-start(bf16[8,16,3072]{2,1,0:T(8,128)(2,1)} %bitcast.104), calls=%async_computation.2 | async-start | bytes 1572864 | tf_op jit(solution)/shard_map/all_to_all | solution.py:147
  351.2 2.0 collective-permute-start
Sparse Core Ops, SparseCore 0:
  9.0 37.4 all-gather.3
  57.4 80.6 all-reduce.1
  253.3 75.6 reduce-scatter.1
where the time goes:
time: 361 us; the launch traced here: 360 us
  waiting for transfers between devices  180 us (50%)
  blocking collectives  96.5 us (27%)
  matrix products  43.1 us (12%)
  between operations  13.4 us (4%)
  local copies, waits for them, and re-layouts  10.7 us (3%)
  other arithmetic  9.6 us (3%)
  starting transfers between devices  7.3 us (2%)
    reduce_scatter x1, waiting for transfers between devices, on_device(): lax.psum_scatter(jnp.dot(hidden, down_w, preferred_element_type=jnp.float...  75.8 us
    all_to_all x1, blocking collectives, on_device(): lax.all_to_all(outgoing, 'exp', split_axis=1, concat_axis=1, tiled=True)  74.1 us
    psum x1, waiting for transfers between devices, on_device(): lax.psum(jnp.dot(mixed, out_weight[0], preferred_element_type=jnp.float32...  54.7 us
    all_gather x1, waiting for transfers between devices, on_device(): sequence = lax.all_gather(inputs[0], 'etp', axis=1, tiled=True)  33.8 us
    all_gather x1, blocking collectives, on_device(): ids_all = lax.all_gather(expert_ids[0], 'etp', axis=0, tiled=True)  22.4 us
    dot_general x1, matrix products, on_device(): jnp.dot(hidden, down_w, preferred_element_type=jnp.float32)  21.6 us
    all_to_all x1, waiting for transfers between devices, on_device(): lax.all_to_all(expert_out.reshape(ep_count, CAP, width), 'exp', split_axi...  13.7 us
    dot_general x1, matrix products, expert_hidden(): upper = jnp.dot(routed_rows, up_w, preferred_element_type=jnp.float32)  10.1 us
  transfers between devices with their start and end apart: 5, of which 5 were waited for; matrix products, arithmetic and copies ran while one was open for 3% of the time, Pallas kernels for 0%

commit v1 on v0

v1 whole, which is shorter than its diff:
```python
import jax
import jax.numpy as jnp
import numpy as np
from jax import lax
from jax.experimental import pallas as pl
from jax.experimental.pallas import tpu as pltpu
from jax.sharding import PartitionSpec as P

D = 3072
HQ = 24
HK = 8
HD = 128
CAP = 16
SEQ = 256
TOK = 32
COLS = D // 8
QKV = 640
HID = 1024
HALF = D // 2

epsilon = 1e-05
rope_base = 1000000.0

MESH = pl.DeviceIdType.MESH
BF = jnp.bfloat16
F32 = jnp.float32

OWN, Z, L, R, LZ, RZ, O, OZ = range(8)
UNITS = (
    (OWN, 0), (OWN, 1), (Z, 0), (L, 1),
    (R, 1), (L, 0), (R, 0), (Z, 1),
    (LZ, 0), (RZ, 0), (LZ, 1), (RZ, 1),
    (O, 1), (O, 0), (OZ, 0), (OZ, 1),
)
UNIT_AT = {unit: i for i, unit in enumerate(UNITS)}
UNIT_ROWS = 64


def rope_tables():
    half = HD // 2
    angles = np.arange(SEQ)[:, None] * rope_base ** (-np.arange(half) / half)[None, :]
    cosine, sine = np.cos(angles), np.sin(angles)
    return (
        np.concatenate([cosine, cosine], axis=1).astype(np.float32),
        np.concatenate([-sine, sine], axis=1).astype(np.float32),
    )


class Gather:
    def __init__(self, copy, at, own, peers):
        left, right, across = peers

        def plan(place, part, half, device, there):
            source = own(part) if place == OWN else at(place, part, half)
            return lambda: copy(source, at(there, part, half), device)

        steps = {
            "a_z": plan(OWN, 0, None, across, Z),
            "a_l": plan(OWN, 0, None, left, R),
            "a_r": plan(OWN, 0, None, right, L),
            "b_z": plan(OWN, 1, None, across, Z),
            "b_l": plan(OWN, 1, None, left, R),
            "b_r": plan(OWN, 1, None, right, L),
            "za_l": plan(Z, 0, None, left, RZ),
            "za_r": plan(Z, 0, None, right, LZ),
            "lb_r": plan(L, 1, 0, right, O),
            "rb_l": plan(R, 1, 1, left, O),
            "lb_z": plan(L, 1, None, across, LZ),
            "rb_z": plan(R, 1, None, across, RZ),
            "la_r": plan(L, 0, 0, right, O),
            "ra_l": plan(R, 0, 1, left, O),
            "lza_r": plan(LZ, 0, 0, right, OZ),
            "rza_l": plan(RZ, 0, 1, left, OZ),
            "ob_z": plan(O, 1, None, across, OZ),
        }
        self.copies = {name: make() for name, make in steps.items()}

    def start(self, *names):
        for name in names:
            self.copies[name].start()

    def arrive(self, *names):
        for name in names:
            self.copies[name].wait_recv()

    def step(self, number):
        if number == 0:
            self.start("b_r", "b_l", "a_z", "a_r", "a_l", "b_z")
        if number == 1:
            self.arrive("b_r")
            self.start("lb_r", "lb_z")
            self.arrive("b_l")
            self.start("rb_l", "rb_z")
            self.arrive("a_z")
            self.start("za_r", "za_l")
        if number == 2:
            self.arrive("a_r", "a_l")
            self.start("la_r", "ra_l")
            self.arrive("lb_r", "rb_l")
            self.start("ob_z")
            self.arrive("b_z")
        if number == 3:
            self.arrive("za_r", "za_l")
            self.start("lza_r", "rza_l")
            self.arrive("lb_z", "rb_z")
        if number == 4:
            self.arrive("la_r", "ra_l", "lza_r", "rza_l", "ob_z")

    def finish(self):
        for one in self.copies.values():
            one.wait_send()


class Reduce:
    def __init__(self, copy, at, buffers, peers):
        left, right, across = peers
        self.at = at
        self.relay_a, self.full_a, self.across_a, self.across_b, self.relay_b, self.full_b = buffers
        self.copies = {
            "oz_r": copy(at(OZ, 0, 0), self.relay_a.at[2], right),
            "oz_l": copy(at(OZ, 0, 1), self.relay_a.at[3], left),
            "o_r": copy(at(O, 0, 0), self.relay_a.at[0], right),
            "o_l": copy(at(O, 0, 1), self.relay_a.at[1], left),
            "rz_r": copy(at(RZ, 0, None), self.full_a.at[2], right),
            "lz_l": copy(at(LZ, 0, None), self.full_a.at[3], left),
            "r_r": copy(at(R, 0, None), self.full_a.at[0], right),
            "l_l": copy(at(L, 0, None), self.full_a.at[1], left),
            "z_z": copy(at(Z, 0, None), self.across_a, across),
            "b_own": copy(at(Z, 1, None), self.across_b.at[0], across),
            "b_left": copy(at(LZ, 1, None), self.across_b.at[1], across),
            "b_right": copy(at(RZ, 1, None), self.across_b.at[2], across),
            "b_opp": copy(at(OZ, 1, None), self.across_b.at[3], across),
            "bo_r": copy(at(O, 1, 0), self.relay_b.at[0], right),
            "bo_l": copy(at(O, 1, 1), self.relay_b.at[1], left),
            "br_r": copy(at(R, 1, None), self.full_b.at[0], right),
            "bl_l": copy(at(L, 1, None), self.full_b.at[1], left),
        }

    def start(self, *names):
        for name in names:
            self.copies[name].start()

    def arrive(self, *names):
        for name in names:
            self.copies[name].wait_recv()

    def add(self, place, part, half, *terms):
        ref = self.at(place, part, half)
        total = ref[...].astype(F32)
        for term in terms:
            total = total + term[...].astype(F32)
        ref[...] = total.astype(BF)

    def early(self):
        self.start("b_left", "b_right", "b_own")

    def run(self):
        self.start("oz_r", "oz_l", "b_opp", "o_r", "o_l")
        self.arrive("oz_r")
        self.add(RZ, 0, 0, self.relay_a.at[2])
        self.start("rz_r")
        self.arrive("oz_l")
        self.add(LZ, 0, 1, self.relay_a.at[3])
        self.start("lz_l")
        self.arrive("b_opp")
        self.add(O, 1, None, self.across_b.at[3])
        self.start("bo_r", "bo_l")
        self.arrive("o_r")
        self.add(R, 0, 0, self.relay_a.at[0])
        self.start("r_r")
        self.arrive("o_l")
        self.add(L, 0, 1, self.relay_a.at[1])
        self.start("l_l")
        self.arrive("b_right", "b_left")
        self.add(R, 1, None, self.across_b.at[2])
        self.add(L, 1, None, self.across_b.at[1])
        self.arrive("bo_r")
        self.add(R, 1, 0, self.relay_b.at[0])
        self.start("br_r")
        self.arrive("bo_l")
        self.add(L, 1, 1, self.relay_b.at[1])
        self.start("bl_l")
        self.arrive("rz_r", "lz_l")
        self.add(Z, 0, None, self.full_a.at[2], self.full_a.at[3])
        self.start("z_z")
        self.arrive("r_r", "l_l", "b_own", "br_r", "bl_l", "z_z")
        part_a = (
            self.at(OWN, 0, None)[...].astype(F32)
            + self.full_a[0].astype(F32)
            + self.full_a[1].astype(F32)
            + self.across_a[...].astype(F32)
        )
        part_b = (
            self.at(OWN, 1, None)[...].astype(F32)
            + self.across_b[0].astype(F32)
            + self.full_b[0].astype(F32)
            + self.full_b[1].astype(F32)
        )
        return part_a, part_b

    def finish(self):
        for one in self.copies.values():
            one.wait_send()


def layer(
    x_ref, gain1_ref, wq_ref, wk_ref, wv_ref, wo_ref, gain2_ref, wg_ref, wu_ref, wd_ref, ids_ref, weights_ref,
    cos_ref, sin_ref, out_ref,
    wqkv, wo, wg, wu, wd, xs, acc, heads, mixed, proj, state, outgoing, rows, act, part, returned, final,
    p_relay_a, p_full_a, p_across_a, p_across_b, p_relay_b, p_full_b,
    d_relay_a, d_full_a, d_across_a, d_across_b, d_relay_b, d_full_b,
    load_sem, send_sem, recv_sem,
):
    pipe, exp, etp = lax.axis_index("pipe"), lax.axis_index("exp"), lax.axis_index("etp")
    zh, y = exp // 4, exp % 4
    zl, x = etp // 4, etp % 4

    def ring(zl_to, step):
        return zl_to * 4 + (x + step) % 4

    index_of = {
        OWN: etp, Z: ring(1 - zl, 0), L: ring(zl, 3), R: ring(zl, 1),
        LZ: ring(1 - zl, 3), RZ: ring(1 - zl, 1), O: ring(zl, 2), OZ: ring(1 - zl, 2),
    }
    peers = tuple((pipe, exp, index_of[place]) for place in (L, R, Z))

    def exchange(dz, dy):
        zh_to, y_to = (zh + dz) % 2, (y + dy) % 4
        return zh_to * 4 + y_to, y_to, (etp if dz == 0 else index_of[Z])

    hops = [(dz, dy) for dy in (2, 1, 3, 0) for dz in (1, 0) if (dz, dy) != (0, 0)]
    other_core = (1 - pipe, exp, etp)

    barrier = pltpu.get_barrier_semaphore()
    for device in peers:
        pl.semaphore_signal(barrier, inc=1, device_id=device, device_id_type=MESH)
    for dz, dy in hops:
        e_to, _, k_to = exchange(dz, dy)
        pl.semaphore_signal(barrier, inc=1, device_id=(pipe, e_to, k_to), device_id_type=MESH)
    pl.semaphore_signal(barrier, inc=1, device_id=other_core, device_id_type=MESH)

    loads = [
        pltpu.make_async_copy(source, target, load_sem.at[i])
        for i, (source, target) in enumerate(
            (
                (x_ref, xs.at[0]),
                (wq_ref, wqkv.at[:, pl.ds(0, 384)]),
                (wk_ref, wqkv.at[:, pl.ds(384, 128)]),
                (wv_ref, wqkv.at[:, pl.ds(512, 128)]),
                (wo_ref, wo),
                (wg_ref, wg),
                (wu_ref, wu),
                (wd_ref, wd),
            )
        )
    ]
    for one in loads:
        one.start()
    pl.semaphore_wait(barrier, 4 + len(hops))

    used = [0]

    def copy(source, target, device):
        i = used[0]
        used[0] = i + 1
        return pltpu.make_async_remote_copy(
            src_ref=source, dst_ref=target, send_sem=send_sem.at[i], recv_sem=recv_sem.at[i],
            device_id=device, device_id_type=MESH,
        )

    def xs_at(place, part_no, half):
        first, count = part_no * 128, 128
        if half is not None:
            first, count = first + half * 64, 64
        return xs.at[place, pl.ds(first, count)]

    features = Gather(copy, xs_at, lambda part_no: x_ref.at[pl.ds(part_no * 128, 128)], peers)
    squares = []

    def project(place):
        offset = pl.multiple_of(index_of[place] * COLS, 128)
        block = xs[place].astype(F32)
        squares.append(jnp.sum(block * block, axis=1, keepdims=True))
        scaled = (block * gain1_ref[:, pl.ds(offset, COLS)].astype(F32)).astype(BF)
        term = jnp.dot(scaled, wqkv[pl.ds(offset, COLS), :], preferred_element_type=F32)
        acc[...] = term if place == OWN else acc[...] + term
        own_rows = pl.ds(pl.multiple_of(etp * TOK, TOK), TOK)
        state[:, pl.ds(offset, COLS)] = xs[place, own_rows, :].astype(F32)

    features.step(0)
    for one in loads[:4]:
        one.wait()
    project(OWN)
    features.step(1)
    features.step(2)
    for place in (Z, L, R):
        project(place)
    features.step(3)
    for place in (LZ, RZ):
        project(place)
    features.step(4)
    for place in (O, OZ):
        project(place)

    factor = lax.rsqrt(sum(squares) * (1.0 / D) + epsilon)
    for i in range(5):
        block = acc[:, i * HD : (i + 1) * HD] * factor
        if i < 4:
            block = block * cos_ref[...] + pltpu.roll(block, HD // 2, 1) * sin_ref[...]
        heads[:, i * HD : (i + 1) * HD] = block.astype(BF)
    causal = lax.broadcasted_iota(jnp.int32, (SEQ, SEQ), 0) >= lax.broadcasted_iota(jnp.int32, (SEQ, SEQ), 1)
    keys, values = heads[:, 384:512], heads[:, 512:640]
    for i in range(3):
        scores = lax.dot_general(
            heads[:, i * HD : (i + 1) * HD], keys, (((1,), (1,)), ((), ())), preferred_element_type=F32
        ) * HD ** (-0.5)
        scores = jnp.where(causal, scores, -1e30)
        expo = jnp.exp(scores - jnp.max(scores, axis=1, keepdims=True))
        probs = (expo / jnp.sum(expo, axis=1, keepdims=True)).astype(BF)
        mixed[:, i * HD : (i + 1) * HD] = jnp.dot(probs, values, preferred_element_type=F32).astype(BF)
    loads[4].wait()

    def out_columns(n, carry):
        columns = pl.ds(pl.multiple_of(n * 512, 512), 512)
        proj[:, columns] = jnp.dot(mixed[...], wo[:, columns], preferred_element_type=F32).astype(BF)
        return carry

    lax.fori_loop(0, D // 512, out_columns, 0)

    def proj_at(place, part_no, half):
        first = pl.multiple_of(index_of[place] * TOK + part_no * 16, 16)
        columns = pl.ds(0, D) if half is None else pl.ds(half * HALF, HALF)
        return proj.at[pl.ds(first, 16), columns]

    attention = Reduce(
        copy, proj_at, (p_relay_a, p_full_a, p_across_a, p_across_b, p_relay_b, p_full_b), peers
    )
    attention.early()

    slot_row = lax.broadcasted_iota(jnp.int32, (8 * CAP, TOK), 0)
    first_route = (ids_ref[0:1, :] == slot_row // CAP).astype(F32)
    second_route = (ids_ref[1:2, :] == slot_row // CAP).astype(F32)
    routed = first_route + second_route
    earlier = (
        lax.broadcasted_iota(jnp.int32, (TOK, TOK), 0) < lax.broadcasted_iota(jnp.int32, (TOK, TOK), 1)
    ).astype(BF)
    before = jnp.dot(routed.astype(BF), earlier, preferred_element_type=F32)
    here = (before == (slot_row % CAP).astype(F32)).astype(F32)
    table = routed * here
    combine = (first_route * weights_ref[0:1, :] + second_route * weights_ref[1:2, :]) * here

    sum_a, sum_b = attention.run()
    state[0:16, :] = (state[0:16, :] + sum_a).astype(BF).astype(F32)
    state[16:32, :] = (state[16:32, :] + sum_b).astype(BF).astype(F32)
    tokens = state[...]
    factor2 = lax.rsqrt(jnp.mean(tokens * tokens, axis=1, keepdims=True) + epsilon)
    ffn_in = (tokens * factor2 * gain2_ref[...].astype(F32)).astype(BF)
    outgoing[...] = jnp.dot(table.astype(BF), ffn_in, preferred_element_type=F32).astype(BF)

    sends = []
    for dz, dy in hops:
        e_to, _, k_to = exchange(dz, dy)
        sends.append(
            copy(
                outgoing.at[pl.ds(pl.multiple_of(e_to * CAP, CAP), CAP)],
                rows.at[pl.ds(pl.multiple_of(dz * UNIT_ROWS + y * CAP, CAP), CAP)],
                (pipe, e_to, k_to),
            )
        )
        sends[-1].start()
    rows[pl.ds(pl.multiple_of(y * CAP, CAP), CAP), :] = outgoing[pl.ds(pl.multiple_of(exp * CAP, CAP), CAP), :]
    for one in sends:
        one.wait_recv()
    for one in loads[5:]:
        one.wait()

    def rows_at(ref):
        def at(place, part_no, half):
            first, count = UNIT_AT[place, part_no] * UNIT_ROWS, UNIT_ROWS
            if half is not None:
                first, count = first + half * (UNIT_ROWS // 2), UNIT_ROWS // 2
            return ref.at[pl.ds(first, count)]

        return at

    def part_at(place, part_no, half):
        columns = pl.ds(0, D) if half is None else pl.ds(half * HALF, HALF)
        return part.at[pl.ds(UNIT_AT[place, part_no] * UNIT_ROWS, UNIT_ROWS), columns]

    dispatch = Gather(copy, rows_at(rows), lambda part_no: rows_at(rows)(OWN, part_no, None), peers)
    shares = Reduce(
        copy, part_at, (d_relay_a, d_full_a, d_across_a, d_across_b, d_relay_b, d_full_b), peers
    )
    dispatch.step(0)

    def expert(group, carry):
        for number in range(4):

            @pl.when(group == number)
            def _(number=number):
                dispatch.step(number + 1)
                if number == 3:
                    shares.early()

        here_rows = pl.ds(pl.multiple_of(group * 256, 256), 256)

        def hidden(n, inner):
            columns = pl.ds(pl.multiple_of(n * 512, 512), 512)
            block = rows[here_rows, :]
            gate = jnp.dot(block, wg[:, columns], preferred_element_type=F32)
            upper = jnp.dot(block, wu[:, columns], preferred_element_type=F32)
            act[:, columns] = (gate / (1.0 + jnp.exp(-gate)) * upper).astype(BF)
            return inner

        lax.fori_loop(0, HID // 512, hidden, 0)

        def down(n, inner):
            columns = pl.ds(pl.multiple_of(n * 512, 512), 512)
            part[here_rows, columns] = jnp.dot(act[...], wd[:, columns], preferred_element_type=F32).astype(BF)
            return inner

        lax.fori_loop(0, D // 512, down, 0)
        return carry

    lax.fori_loop(0, 4, expert, 0)

    sum_a, sum_b = shares.run()
    final[0:UNIT_ROWS, :] = sum_a.astype(BF)
    final[UNIT_ROWS:, :] = sum_b.astype(BF)

    own_slots = pl.ds(pl.multiple_of(exp * CAP, CAP), CAP)
    backs = []
    for dz, dy in hops:
        e_to, y_to, k_to = exchange(dz, dy)
        backs.append(
            copy(
                final.at[pl.ds(pl.multiple_of(dz * UNIT_ROWS + y_to * CAP, CAP), CAP)],
                returned.at[own_slots],
                (pipe, e_to, k_to),
            )
        )
        backs[-1].start()
    returned[own_slots, :] = final[pl.ds(pl.multiple_of(y * CAP, CAP), CAP), :]
    combine_high = combine.astype(BF)
    combine_low = (combine - combine_high.astype(F32)).astype(BF)
    for one in backs:
        one.wait_recv()
    over_slots = (((0,), (0,)), ((), ()))
    moe = lax.dot_general(combine_high, returned[...], over_slots, preferred_element_type=F32)
    moe = moe + lax.dot_general(combine_low, returned[...], over_slots, preferred_element_type=F32)
    state[...] = state[...] + moe
    outgoing_final = final.at[pl.ds(0, TOK)]
    for one in backs:
        one.wait_send()
    outgoing_final[...] = state[...].astype(BF)
    handed = copy(outgoing_final, out_ref, other_core)
    handed.start()
    for one in (features, attention, dispatch, shares):
        one.finish()
    for one in sends:
        one.wait_send()
    handed.wait()


def buffers(part_rows):
    return [
        pltpu.VMEM((4, part_rows, HALF), BF),
        pltpu.VMEM((4, part_rows, D), BF),
        pltpu.VMEM((part_rows, D), BF),
        pltpu.VMEM((4, part_rows, D), BF),
        pltpu.VMEM((2, part_rows, HALF), BF),
        pltpu.VMEM((2, part_rows, D), BF),
    ]


def on_device(
    inputs,
    attn_gain,
    query_weight,
    key_weight,
    value_weight,
    out_weight,
    ffn_gain,
    gate_weight,
    up_weight,
    down_weight,
    expert_ids,
    route_weights,
):
    cosine, sine = rope_tables()
    anywhere = pl.BlockSpec(memory_space=pl.ANY)
    vmem = pl.BlockSpec(memory_space=pltpu.VMEM)
    handed = pl.pallas_call(
        layer,
        out_shape=jax.ShapeDtypeStruct((TOK, D), BF),
        in_specs=[anywhere, vmem] + [anywhere] * 4 + [vmem] + [anywhere] * 3 + [vmem] * 4,
        out_specs=anywhere,
        scratch_shapes=[
            pltpu.VMEM((D, QKV), BF),
            pltpu.VMEM((384, D), BF),
            pltpu.VMEM((D, HID), BF),
            pltpu.VMEM((D, HID), BF),
            pltpu.VMEM((HID, D), BF),
            pltpu.VMEM((8, SEQ, COLS), BF),
            pltpu.VMEM((SEQ, QKV), F32),
            pltpu.VMEM((SEQ, QKV), BF),
            pltpu.VMEM((SEQ, 384), BF),
            pltpu.VMEM((SEQ, D), BF),
            pltpu.VMEM((TOK, D), F32),
            pltpu.VMEM((8 * CAP, D), BF),
            pltpu.VMEM((16 * UNIT_ROWS, D), BF),
            pltpu.VMEM((256, HID), BF),
            pltpu.VMEM((16 * UNIT_ROWS, D), BF),
            pltpu.VMEM((8 * CAP, D), BF),
            pltpu.VMEM((2 * UNIT_ROWS, D), BF),
            *buffers(16),
            *buffers(UNIT_ROWS),
            pltpu.SemaphoreType.DMA((8,)),
            pltpu.SemaphoreType.DMA((96,)),
            pltpu.SemaphoreType.DMA((96,)),
        ],
        compiler_params=pltpu.CompilerParams(
            collective_id=0, has_side_effects=True, vmem_limit_bytes=60 * 2**20
        ),
        cost_estimate=pl.CostEstimate(flops=22_000_000_000, bytes_accessed=26_000_000, transcendentals=0),
        name="layer",
    )(
        inputs[0],
        attn_gain,
        query_weight[0],
        key_weight[0],
        value_weight[0],
        out_weight[0],
        ffn_gain,
        gate_weight[0, 0],
        up_weight[0, 0],
        down_weight[0, 0],
        expert_ids[0].T,
        route_weights[0].T,
        jnp.asarray(cosine),
        jnp.asarray(sine),
    )
    return handed[None]


def solution(mesh):
    in_specs = (
        P("pipe", "exp", "etp"),
        P("pipe", None),
        P("pipe", None, "etp"),
        P("pipe", None, "etp"),
        P("pipe", None, "etp"),
        P("pipe", "etp", None),
        P("pipe", None),
        P("pipe", "exp", None, "etp"),
        P("pipe", "exp", None, "etp"),
        P("pipe", "exp", "etp", None),
        P("pipe", ("exp", "etp"), None),
        P("pipe", ("exp", "etp"), None),
    )
    out_specs = P("pipe", ("exp", "etp"), None)
    return jax.shard_map(
        on_device, mesh=mesh, in_specs=in_specs, out_specs=out_specs, check_vma=False
    )
```

time: 361 us -> 161 us (0.45)
  waiting for transfers between devices: 180 us -> 0 us
  Pallas kernels: 0 us -> 159 us
  blocking collectives: 96.5 us -> 0 us
  matrix products: 43.1 us -> 0 us
  between operations: 13.4 us -> 0.01 us
  other arithmetic: 9.6 us -> 0 us
  local copies, waits for them, and re-layouts: 10.7 us -> 1.62 us
  starting transfers between devices: 7.3 us -> 0 us
    pallas_call x0 -> x1, Pallas kernels: none -> 159 us  [on_device(): pl.pallas_call(layer, out_shape=jax.ShapeDtypeStruct((TOK, D), BF), in_sp...]
    reduce_scatter x1 -> x0, waiting for transfers between devices: 75.8 us -> none  [on_device(): lax.psum_scatter(jnp.dot(hidden, down_w, preferred_element_type=jnp.float...]
    all_to_all x1 -> x0, blocking collectives: 74.1 us -> none  [on_device(): lax.all_to_all(outgoing, 'exp', split_axis=1, concat_axis=1, tiled=True)]
    psum x1 -> x0, waiting for transfers between devices: 54.7 us -> none  [on_device(): lax.psum(jnp.dot(mixed, out_weight[0], preferred_element_type=jnp.float32...]
    dot_general x9 -> x0, matrix products: 43.1 us -> none  [the longest x1 21.6 us: on_device(): jnp.dot(hidden, down_w, preferred_element_type=jnp.float32)]
    all_gather x1 -> x0, waiting for transfers between devices: 33.8 us -> none  [on_device(): sequence = lax.all_gather(inputs[0], 'etp', axis=1, tiled=True)]
    all_gather x1 -> x0, blocking collectives: 22.4 us -> none  [on_device(): ids_all = lax.all_gather(expert_ids[0], 'etp', axis=0, tiled=True)]
    all_to_all x1 -> x0, waiting for transfers between devices: 13.7 us -> none  [on_device(): lax.all_to_all(expert_out.reshape(ep_count, CAP, width), 'exp', split_axi...]
  transfers between devices with their start and end apart: 5 -> 0, of which waited for: 5 -> 0; matrix products, arithmetic and copies ran while one was open for 3% -> 0% of each run, Pallas kernels for 0% -> 0%
where the time goes in v1:
time: 161 us; the launch traced here: 160 us
  Pallas kernels  159 us (99%)
  local copies, waits for them, and re-layouts  1.62 us (1%)
    pallas_call x1, Pallas kernels, on_device(): pl.pallas_call(layer, out_shape=jax.ShapeDtypeStruct((TOK, D), BF), in_sp...  159 us

profile of v1, /device:TPU:1, one launch (start us, length us, event | category | flops | bytes accessed | tf_op | source)
XLA Modules:
  0.0 160.3 jit_solution(2191672513872303567)
XLA Ops:
  0.0 158.6 %layer.1 = bf16[32,3072]{1,0:T(8,128)(2,1)} custom-call(bf16[256,384]{1,0:T(8,128)(2,1)} %bitcast.23, bf16[1,3072]{1,0:T(2,128)(2,1)} %gain1_ref.1, bf16[3072,384]{1,0:T(8,128)(2,1)} %bitcast.19, bf16[3072,128]{1,0:T(8,128)(2,1)} %bitcast.21, bf16[3072,128]{1,0:T(8,128)(2,1)} %bitcast.22, bf16[384,3072]{1,0:T(8,128)(2,1)} %bitcast.20, ...), custom_call_target="tpu_custom_call" | custom-call | flops 22000001024 | bytes 26000000 | tf_op jit(solution)/shard_map/layer/pallas_call | solution.py:493
  158.6 1.6 %copy.16 = bf16[1,32,3072]{2,1,0:T(8,128)(2,1)} copy(bf16[1,32,3072]{2,1,0:T(8,128)(2,1)} %bitcast.15) | data formatting | bytes 393216

commit v2 on v1

--- a/solution.py
+++ b/solution.py
@@ -16,7 +16,6 @@
 COLS = D // 8
 QKV = 640
 HID = 1024
-HALF = D // 2
 
 epsilon = 1e-05
 rope_base = 1000000.0
@@ -26,14 +25,12 @@
 F32 = jnp.float32
 
 OWN, Z, L, R, LZ, RZ, O, OZ = range(8)
-UNITS = (
-    (OWN, 0), (OWN, 1), (Z, 0), (L, 1),
-    (R, 1), (L, 0), (R, 0), (Z, 1),
-    (LZ, 0), (RZ, 0), (LZ, 1), (RZ, 1),
-    (O, 1), (O, 0), (OZ, 0), (OZ, 1),
-)
-UNIT_AT = {unit: i for i, unit in enumerate(UNITS)}
-UNIT_ROWS = 64
+SLOTS = 8 * CAP
+PART_SLOTS = SLOTS // 2
+SPLIT = 2048
+SPLIT_BACK = 2048
+META = 16
+X_ROWS = SEQ + META
 
 
 def rope_tables():
@@ -47,12 +44,11 @@
 
 
 class Gather:
-    def __init__(self, copy, at, own, peers):
+    def __init__(self, copy, at, peers):
         left, right, across = peers
 
         def plan(place, part, half, device, there):
-            source = own(part) if place == OWN else at(place, part, half)
-            return lambda: copy(source, at(there, part, half), device)
+            return lambda: copy(at(place, part, half), at(there, part, half), device)
 
         steps = {
             "a_z": plan(OWN, 0, None, across, Z),
@@ -93,12 +89,12 @@
             self.start("rb_l", "rb_z")
             self.arrive("a_z")
             self.start("za_r", "za_l")
+            self.arrive("b_z")
         if number == 2:
             self.arrive("a_r", "a_l")
             self.start("la_r", "ra_l")
             self.arrive("lb_r", "rb_l")
             self.start("ob_z")
-            self.arrive("b_z")
         if number == 3:
             self.arrive("za_r", "za_l")
             self.start("lza_r", "rza_l")
@@ -156,21 +152,25 @@
 
     def run(self):
         self.start("oz_r", "oz_l", "b_opp", "o_r", "o_l")
+        yield
         self.arrive("oz_r")
         self.add(RZ, 0, 0, self.relay_a.at[2])
         self.start("rz_r")
         self.arrive("oz_l")
         self.add(LZ, 0, 1, self.relay_a.at[3])
         self.start("lz_l")
+        yield
         self.arrive("b_opp")
         self.add(O, 1, None, self.across_b.at[3])
         self.start("bo_r", "bo_l")
+        yield
         self.arrive("o_r")
         self.add(R, 0, 0, self.relay_a.at[0])
         self.start("r_r")
         self.arrive("o_l")
         self.add(L, 0, 1, self.relay_a.at[1])
         self.start("l_l")
+        yield
         self.arrive("b_right", "b_left")
         self.add(R, 1, None, self.across_b.at[2])
         self.add(L, 1, None, self.across_b.at[1])
@@ -180,35 +180,58 @@
         self.arrive("bo_l")
         self.add(L, 1, 1, self.relay_b.at[1])
         self.start("bl_l")
+        yield
         self.arrive("rz_r", "lz_l")
         self.add(Z, 0, None, self.full_a.at[2], self.full_a.at[3])
         self.start("z_z")
-        self.arrive("r_r", "l_l", "b_own", "br_r", "bl_l", "z_z")
-        part_a = (
-            self.at(OWN, 0, None)[...].astype(F32)
-            + self.full_a[0].astype(F32)
-            + self.full_a[1].astype(F32)
-            + self.across_a[...].astype(F32)
-        )
+        yield
+        self.arrive("r_r", "l_l", "b_own", "br_r", "bl_l")
         part_b = (
             self.at(OWN, 1, None)[...].astype(F32)
             + self.across_b[0].astype(F32)
             + self.full_b[0].astype(F32)
             + self.full_b[1].astype(F32)
         )
-        return part_a, part_b
+        part_a = (
+            self.at(OWN, 0, None)[...].astype(F32)
+            + self.full_a[0].astype(F32)
+            + self.full_a[1].astype(F32)
+        )
+        self.arrive("z_z")
+        self.sums = part_a + self.across_a[...].astype(F32), part_b
 
     def finish(self):
         for one in self.copies.values():
             one.wait_send()
 
 
+def placed(first_ids, second_ids):
+    slot_row = lax.broadcasted_iota(jnp.int32, (SLOTS, TOK), 0)
+    expert = (slot_row // CAP).astype(F32)
+    first_route = (first_ids == expert).astype(F32)
+    second_route = (second_ids == expert).astype(F32)
+    earlier = (
+        lax.broadcasted_iota(jnp.int32, (TOK, TOK), 0) < lax.broadcasted_iota(jnp.int32, (TOK, TOK), 1)
+    ).astype(BF)
+    before = jnp.dot((first_route + second_route).astype(BF), earlier, preferred_element_type=F32)
+    here = (before == (slot_row % CAP).astype(F32)).astype(F32)
+    return first_route * here, second_route * here
+
+
+def split_in_three(values):
+    high = values.astype(BF).astype(F32)
+    middle = (values - high).astype(BF).astype(F32)
+    return high, middle, values - high - middle
+
+
 def layer(
     x_ref, gain1_ref, wq_ref, wk_ref, wv_ref, wo_ref, gain2_ref, wg_ref, wu_ref, wd_ref, ids_ref, weights_ref,
     cos_ref, sin_ref, out_ref,
-    wqkv, wo, wg, wu, wd, xs, acc, heads, mixed, proj, state, outgoing, rows, act, part, returned, final,
+    wqkv, wo, wg, wu, wd, xs, acc, heads, mixed, proj, state, tables, combine, outgoing, tokens, wide_out, rows, act,
+    part, final, returned, wide_back, moe, handed,
     p_relay_a, p_full_a, p_across_a, p_across_b, p_relay_b, p_full_b,
     d_relay_a, d_full_a, d_across_a, d_across_b, d_relay_b, d_full_b,
+    m_relay_a, m_full_a, m_across_a, m_across_b, m_relay_b, m_full_b,
     load_sem, send_sem, recv_sem,
 ):
     pipe, exp, etp = lax.axis_index("pipe"), lax.axis_index("exp"), lax.axis_index("etp")
@@ -243,7 +266,7 @@
         pltpu.make_async_copy(source, target, load_sem.at[i])
         for i, (source, target) in enumerate(
             (
-                (x_ref, xs.at[0]),
+                (x_ref, xs.at[0, pl.ds(0, SEQ)]),
                 (wq_ref, wqkv.at[:, pl.ds(0, 384)]),
                 (wk_ref, wqkv.at[:, pl.ds(384, 128)]),
                 (wv_ref, wqkv.at[:, pl.ds(512, 128)]),
@@ -256,6 +279,16 @@
     ]
     for one in loads:
         one.start()
+
+    xs[0, SEQ:X_ROWS, :] = jnp.zeros((META, COLS), BF)
+    meta_row = lax.broadcasted_iota(jnp.int32, (META, TOK), 0)
+    meta_rows = [ids_ref[0:1, :].astype(F32), ids_ref[1:2, :].astype(F32)]
+    meta_rows += [*split_in_three(weights_ref[0:1, :]), *split_in_three(weights_ref[1:2, :])]
+    meta = jnp.zeros((META, TOK), F32)
+    for i, row in enumerate(meta_rows):
+        meta = jnp.where(meta_row == i, row, meta)
+    xs[0, SEQ:X_ROWS, 0:TOK] = meta.astype(BF)
+    loads[0].wait()
     pl.semaphore_wait(barrier, 4 + len(hops))
 
     used = [0]
@@ -268,18 +301,20 @@
             device_id=device, device_id_type=MESH,
         )
 
+    x_parts = {
+        (0, None): (0, 144), (0, 0): (0, 80), (0, 1): (80, 64),
+        (1, None): (144, 128), (1, 0): (144, 64), (1, 1): (208, 64),
+    }
+
     def xs_at(place, part_no, half):
-        first, count = part_no * 128, 128
-        if half is not None:
-            first, count = first + half * 64, 64
-        return xs.at[place, pl.ds(first, count)]
-
-    features = Gather(copy, xs_at, lambda part_no: x_ref.at[pl.ds(part_no * 128, 128)], peers)
+        return xs.at[place, pl.ds(*x_parts[part_no, half])]
+
+    features = Gather(copy, xs_at, peers)
     squares = []
 
     def project(place):
         offset = pl.multiple_of(index_of[place] * COLS, 128)
-        block = xs[place].astype(F32)
+        block = xs[place, 0:SEQ, :].astype(F32)
         squares.append(jnp.sum(block * block, axis=1, keepdims=True))
         scaled = (block * gain1_ref[:, pl.ds(offset, COLS)].astype(F32)).astype(BF)
         term = jnp.dot(scaled, wqkv[pl.ds(offset, COLS), :], preferred_element_type=F32)
@@ -288,7 +323,7 @@
         state[:, pl.ds(offset, COLS)] = xs[place, own_rows, :].astype(F32)
 
     features.step(0)
-    for one in loads[:4]:
+    for one in loads[1:4]:
         one.wait()
     project(OWN)
     features.step(1)
@@ -329,69 +364,138 @@
 
     def proj_at(place, part_no, half):
         first = pl.multiple_of(index_of[place] * TOK + part_no * 16, 16)
-        columns = pl.ds(0, D) if half is None else pl.ds(half * HALF, HALF)
+        columns = pl.ds(0, D) if half is None else pl.ds(half * (D // 2), D // 2)
         return proj.at[pl.ds(first, 16), columns]
 
     attention = Reduce(
         copy, proj_at, (p_relay_a, p_full_a, p_across_a, p_across_b, p_relay_b, p_full_b), peers
     )
     attention.early()
-
-    slot_row = lax.broadcasted_iota(jnp.int32, (8 * CAP, TOK), 0)
-    first_route = (ids_ref[0:1, :] == slot_row // CAP).astype(F32)
-    second_route = (ids_ref[1:2, :] == slot_row // CAP).astype(F32)
-    routed = first_route + second_route
-    earlier = (
-        lax.broadcasted_iota(jnp.int32, (TOK, TOK), 0) < lax.broadcasted_iota(jnp.int32, (TOK, TOK), 1)
-    ).astype(BF)
-    before = jnp.dot(routed.astype(BF), earlier, preferred_element_type=F32)
-    here = (before == (slot_row % CAP).astype(F32)).astype(F32)
-    table = routed * here
-    combine = (first_route * weights_ref[0:1, :] + second_route * weights_ref[1:2, :]) * here
-
-    sum_a, sum_b = attention.run()
+    running = attention.run()
+    next(running)
+
+    for place in range(8):
+        sent = xs[place, SEQ:X_ROWS, 0:TOK].astype(F32)
+        first_route, second_route = placed(sent[0:1], sent[1:2])
+        tables[place] = (first_route + second_route).astype(BF)
+        weight = first_route * (sent[2:3] + sent[3:4] + sent[4:5])
+        weight = weight + second_route * (sent[5:6] + sent[6:7] + sent[7:8])
+        high = weight.astype(BF)
+        combine[0, place] = high
+        combine[1, place] = (weight - high.astype(F32)).astype(BF)
+
+    def combined(place, outputs):
+        over_slots = (((0,), (0,)), ((), ()))
+        total = lax.dot_general(combine[0, place], outputs, over_slots, preferred_element_type=F32)
+        return total + lax.dot_general(combine[1, place], outputs, over_slots, preferred_element_type=F32)
+
+    for _ in running:
+        pass
+    sum_a, sum_b = attention.sums
     state[0:16, :] = (state[0:16, :] + sum_a).astype(BF).astype(F32)
     state[16:32, :] = (state[16:32, :] + sum_b).astype(BF).astype(F32)
-    tokens = state[...]
-    factor2 = lax.rsqrt(jnp.mean(tokens * tokens, axis=1, keepdims=True) + epsilon)
-    ffn_in = (tokens * factor2 * gain2_ref[...].astype(F32)).astype(BF)
-    outgoing[...] = jnp.dot(table.astype(BF), ffn_in, preferred_element_type=F32).astype(BF)
-
+    state_now = state[...]
+    factor2 = lax.rsqrt(jnp.mean(state_now * state_now, axis=1, keepdims=True) + epsilon)
+    ffn_in = (state_now * factor2 * gain2_ref[...].astype(F32)).astype(BF)
+
+    tokens[OWN] = ffn_in[:, SPLIT:]
+
+    def halves_at(ref, first_rows, rows_each, first_columns, width):
+        def at(place, part_no, half):
+            columns = pl.ds(first_columns, width)
+            if half is not None:
+                columns = pl.ds(first_columns + half * (width // 2), width // 2)
+            return ref.at[place, pl.ds(first_rows + part_no * rows_each, rows_each), columns]
+
+        return at
+
+    spread = Gather(copy, halves_at(tokens, 0, 16, 0, D - SPLIT), peers)
+    spread.step(0)
+
+    outgoing[...] = jnp.dot(tables[OWN], ffn_in[:, :SPLIT], preferred_element_type=F32).astype(BF)
     sends = []
     for dz, dy in hops:
         e_to, _, k_to = exchange(dz, dy)
         sends.append(
             copy(
                 outgoing.at[pl.ds(pl.multiple_of(e_to * CAP, CAP), CAP)],
-                rows.at[pl.ds(pl.multiple_of(dz * UNIT_ROWS + y * CAP, CAP), CAP)],
+                rows.at[OWN, pl.ds(pl.multiple_of(dz * PART_SLOTS + y * CAP, CAP), CAP), pl.ds(0, SPLIT)],
                 (pipe, e_to, k_to),
             )
         )
         sends[-1].start()
-    rows[pl.ds(pl.multiple_of(y * CAP, CAP), CAP), :] = outgoing[pl.ds(pl.multiple_of(exp * CAP, CAP), CAP), :]
+    own_slots = pl.ds(pl.multiple_of(exp * CAP, CAP), CAP)
+    own_block = pl.ds(pl.multiple_of(y * CAP, CAP), CAP)
+    rows[OWN, own_block, 0:SPLIT] = outgoing[own_slots, :]
+
+    wide_sends = []
+
+    def widen(group):
+        for place in (2 * group, 2 * group + 1):
+            block = jnp.dot(tables[place], tokens[place], preferred_element_type=F32).astype(BF)
+            wide_out[:, place] = block.reshape(8, CAP, D - SPLIT)
+        copies = []
+        for dz, dy in hops:
+            e_to, _, k_to = exchange(dz, dy)
+            copies.append(
+                copy(
+                    wide_out.at[e_to, pl.ds(2 * group, 2)],
+                    rows.at[
+                        pl.ds(2 * group, 2),
+                        pl.ds(pl.multiple_of(dz * PART_SLOTS + y * CAP, CAP), CAP),
+                        pl.ds(SPLIT, D - SPLIT),
+                    ],
+                    (pipe, e_to, k_to),
+                )
+            )
+            copies[-1].start()
+        for place in (2 * group, 2 * group + 1):
+            rows[place, own_block, SPLIT:] = wide_out[exp, place]
+        wide_sends.append(copies)
+
+    spread.step(1)
+    widen(0)
+    spread.step(2)
+    widen(1)
+    spread.step(3)
+    widen(2)
+    spread.step(4)
+    widen(3)
+
+    dispatch = Gather(copy, lambda place, part_no, half: rows.at[
+        place,
+        pl.ds(part_no * PART_SLOTS + (half or 0) * (PART_SLOTS // 2), PART_SLOTS // (1 if half is None else 2)),
+        pl.ds(0, SPLIT),
+    ], peers)
+    shares = Reduce(
+        copy,
+        halves_at(part, 0, PART_SLOTS, 0, SPLIT_BACK),
+        (d_relay_a, d_full_a, d_across_a, d_across_b, d_relay_b, d_full_b),
+        peers,
+    )
+    wide_backs = []
+    for group in range(4):
+        copies = []
+        for dz, dy in hops:
+            e_to, y_to, k_to = exchange(dz, dy)
+            copies.append(
+                copy(
+                    part.at[
+                        pl.ds(2 * group, 2),
+                        pl.ds(pl.multiple_of(dz * PART_SLOTS + y_to * CAP, CAP), CAP),
+                        pl.ds(SPLIT_BACK, D - SPLIT_BACK),
+                    ],
+                    wide_back.at[pl.ds(2 * group, 2), own_slots],
+                    (pipe, e_to, k_to),
+                )
+            )
+        wide_backs.append(copies)
+
     for one in sends:
         one.wait_recv()
+    dispatch.step(0)
     for one in loads[5:]:
         one.wait()
-
-    def rows_at(ref):
-        def at(place, part_no, half):
-            first, count = UNIT_AT[place, part_no] * UNIT_ROWS, UNIT_ROWS
-            if half is not None:
-                first, count = first + half * (UNIT_ROWS // 2), UNIT_ROWS // 2
-            return ref.at[pl.ds(first, count)]
-
-        return at
-
-    def part_at(place, part_no, half):
-        columns = pl.ds(0, D) if half is None else pl.ds(half * HALF, HALF)
-        return part.at[pl.ds(UNIT_AT[place, part_no] * UNIT_ROWS, UNIT_ROWS), columns]
-
-    dispatch = Gather(copy, rows_at(rows), lambda part_no: rows_at(rows)(OWN, part_no, None), peers)
-    shares = Reduce(
-        copy, part_at, (d_relay_a, d_full_a, d_across_a, d_across_b, d_relay_b, d_full_b), peers
-    )
-    dispatch.step(0)
 
     def expert(group, carry):
         for number in range(4):
@@ -399,14 +503,16 @@
             @pl.when(group == number)
             def _(number=number):
                 dispatch.step(number + 1)
+                for one in wide_sends[number]:
+                    one.wait_recv()
                 if number == 3:
                     shares.early()
 
-        here_rows = pl.ds(pl.multiple_of(group * 256, 256), 256)
+        places = pl.ds(group * 2, 2)
 
         def hidden(n, inner):
             columns = pl.ds(pl.multiple_of(n * 512, 512), 512)
-            block = rows[here_rows, :]
+            block = rows[places].reshape(2 * SLOTS, D)
             gate = jnp.dot(block, wg[:, columns], preferred_element_type=F32)
             upper = jnp.dot(block, wu[:, columns], preferred_element_type=F32)
             act[:, columns] = (gate / (1.0 + jnp.exp(-gate)) * upper).astype(BF)
@@ -416,60 +522,89 @@
 
         def down(n, inner):
             columns = pl.ds(pl.multiple_of(n * 512, 512), 512)
-            part[here_rows, columns] = jnp.dot(act[...], wd[:, columns], preferred_element_type=F32).astype(BF)
+            block = jnp.dot(act[...], wd[:, columns], preferred_element_type=F32).astype(BF)
+            part[places, :, columns] = block.reshape(2, SLOTS, 512)
             return inner
 
         lax.fori_loop(0, D // 512, down, 0)
+        for number in range(4):
+
+            @pl.when(group == number)
+            def _(number=number):
+                for one in wide_backs[number]:
+                    one.start()
+                for place in (2 * number, 2 * number + 1):
+                    wide_back[place, own_slots, :] = part[place, own_block, SPLIT_BACK:]
+
         return carry
 
     lax.fori_loop(0, 4, expert, 0)
 
-    sum_a, sum_b = shares.run()
-    final[0:UNIT_ROWS, :] = sum_a.astype(BF)
-    final[UNIT_ROWS:, :] = sum_b.astype(BF)
-
-    own_slots = pl.ds(pl.multiple_of(exp * CAP, CAP), CAP)
+    sums = Reduce(
+        copy,
+        halves_at(moe, 0, 16, 0, D - SPLIT_BACK),
+        (m_relay_a, m_full_a, m_across_a, m_across_b, m_relay_b, m_full_b),
+        peers,
+    )
+    narrow, wide = shares.run(), sums.run()
+    for _ in range(4):
+        next(narrow)
+    for group in range(4):
+        for one in wide_backs[group]:
+            one.wait_recv()
+        for place in (2 * group, 2 * group + 1):
+            moe[place] = combined(place, wide_back[place]).astype(BF)
+    sums.early()
+    next(wide)
+    next(narrow)
+    next(wide)
+    next(wide)
+    next(narrow)
+    for _ in range(3):
+        next(wide)
+    for _ in narrow:
+        pass
+    sum_a, sum_b = shares.sums
+    final[0:PART_SLOTS, :] = sum_a.astype(BF)
+    final[PART_SLOTS:, :] = sum_b.astype(BF)
+
     backs = []
     for dz, dy in hops:
         e_to, y_to, k_to = exchange(dz, dy)
         backs.append(
             copy(
-                final.at[pl.ds(pl.multiple_of(dz * UNIT_ROWS + y_to * CAP, CAP), CAP)],
+                final.at[pl.ds(pl.multiple_of(dz * PART_SLOTS + y_to * CAP, CAP), CAP)],
                 returned.at[own_slots],
                 (pipe, e_to, k_to),
             )
         )
         backs[-1].start()
-    returned[own_slots, :] = final[pl.ds(pl.multiple_of(y * CAP, CAP), CAP), :]
-    combine_high = combine.astype(BF)
-    combine_low = (combine - combine_high.astype(F32)).astype(BF)
+    returned[own_slots, :] = final[own_block, :]
+    for _ in wide:
+        pass
+    sum_a, sum_b = sums.sums
+    handed[0:16, SPLIT_BACK:] = (state[0:16, SPLIT_BACK:] + sum_a).astype(BF)
+    handed[16:32, SPLIT_BACK:] = (state[16:32, SPLIT_BACK:] + sum_b).astype(BF)
     for one in backs:
         one.wait_recv()
-    over_slots = (((0,), (0,)), ((), ()))
-    moe = lax.dot_general(combine_high, returned[...], over_slots, preferred_element_type=F32)
-    moe = moe + lax.dot_general(combine_low, returned[...], over_slots, preferred_element_type=F32)
-    state[...] = state[...] + moe
-    outgoing_final = final.at[pl.ds(0, TOK)]
-    for one in backs:
+    handed[:, :SPLIT_BACK] = (state[:, :SPLIT_BACK] + combined(OWN, returned[...])).astype(BF)
+    handing = copy(handed, out_ref, other_core)
+    handing.start()
+    for one in (features, attention, spread, dispatch, shares, sums):
+        one.finish()
+    for one in sum(wide_sends + wide_backs, sends + backs):
         one.wait_send()
-    outgoing_final[...] = state[...].astype(BF)
-    handed = copy(outgoing_final, out_ref, other_core)
-    handed.start()
-    for one in (features, attention, dispatch, shares):
-        one.finish()
-    for one in sends:
-        one.wait_send()
-    handed.wait()
-
-
-def buffers(part_rows):
+    handing.wait()
+
+
+def buffers(part_rows, width):
     return [
-        pltpu.VMEM((4, part_rows, HALF), BF),
-        pltpu.VMEM((4, part_rows, D), BF),
-        pltpu.VMEM((part_rows, D), BF),
-        pltpu.VMEM((4, part_rows, D), BF),
-        pltpu.VMEM((2, part_rows, HALF), BF),
-        pltpu.VMEM((2, part_rows, D), BF),
+        pltpu.VMEM((4, part_rows, width // 2), BF),
+        pltpu.VMEM((4, part_rows, width), BF),
+        pltpu.VMEM((part_rows, width), BF),
+        pltpu.VMEM((4, part_rows, width), BF),
+        pltpu.VMEM((2, part_rows, width // 2), BF),
+        pltpu.VMEM((2, part_rows, width), BF),
     ]
 
 
@@ -501,23 +636,31 @@
             pltpu.VMEM((D, HID), BF),
             pltpu.VMEM((D, HID), BF),
             pltpu.VMEM((HID, D), BF),
-            pltpu.VMEM((8, SEQ, COLS), BF),
+            pltpu.VMEM((8, X_ROWS, COLS), BF),
             pltpu.VMEM((SEQ, QKV), F32),
             pltpu.VMEM((SEQ, QKV), BF),
             pltpu.VMEM((SEQ, 384), BF),
             pltpu.VMEM((SEQ, D), BF),
             pltpu.VMEM((TOK, D), F32),
-            pltpu.VMEM((8 * CAP, D), BF),
-            pltpu.VMEM((16 * UNIT_ROWS, D), BF),
-            pltpu.VMEM((256, HID), BF),
-            pltpu.VMEM((16 * UNIT_ROWS, D), BF),
-            pltpu.VMEM((8 * CAP, D), BF),
-            pltpu.VMEM((2 * UNIT_ROWS, D), BF),
-            *buffers(16),
-            *buffers(UNIT_ROWS),
+            pltpu.VMEM((8, SLOTS, TOK), BF),
+            pltpu.VMEM((2, 8, SLOTS, TOK), BF),
+            pltpu.VMEM((SLOTS, SPLIT), BF),
+            pltpu.VMEM((8, TOK, D - SPLIT), BF),
+            pltpu.VMEM((8, 8, CAP, D - SPLIT), BF),
+            pltpu.VMEM((8, SLOTS, D), BF),
+            pltpu.VMEM((2 * SLOTS, HID), BF),
+            pltpu.VMEM((8, SLOTS, D), BF),
+            pltpu.VMEM((SLOTS, SPLIT_BACK), BF),
+            pltpu.VMEM((SLOTS, SPLIT_BACK), BF),
+            pltpu.VMEM((8, SLOTS, D - SPLIT_BACK), BF),
+            pltpu.VMEM((8, TOK, D - SPLIT_BACK), BF),
+            pltpu.VMEM((TOK, D), BF),
+            *buffers(16, D),
+            *buffers(PART_SLOTS, SPLIT_BACK),
+            *buffers(16, D - SPLIT_BACK),
             pltpu.SemaphoreType.DMA((8,)),
-            pltpu.SemaphoreType.DMA((96,)),
-            pltpu.SemaphoreType.DMA((96,)),
+            pltpu.SemaphoreType.DMA((174,)),
+            pltpu.SemaphoreType.DMA((174,)),
         ],
         compiler_params=pltpu.CompilerParams(
             collective_id=0, has_side_effects=True, vmem_limit_bytes=60 * 2**20

time: 161 us -> 131 us (0.81)
  Pallas kernels: 159 us -> 129 us
    pallas_call x1, Pallas kernels: 159 us -> 129 us  [on_device(): pl.pallas_call(layer, out_shape=jax.ShapeDtypeStruct((TOK, D), BF), in_sp...]
where the time goes in v2:
time: 131 us
  Pallas kernels  129 us (98%)
  local copies, waits for them, and re-layouts  1.62 us (1%)
    pallas_call x1, Pallas kernels, on_device(): pl.pallas_call(layer, out_shape=jax.ShapeDtypeStruct((TOK, D), BF), in_sp...  129 us

profile of v2, /device:TPU:1, one launch (start us, length us, event | category | flops | bytes accessed | tf_op | source)
XLA Modules:
  0.0 130.8 jit_solution(9698617458077836018)
XLA Ops:
  0.0 129.2 %layer.1 = bf16[32,3072]{1,0:T(8,128)(2,1)} custom-call(bf16[256,384]{1,0:T(8,128)(2,1)} %bitcast.23, bf16[1,3072]{1,0:T(2,128)(2,1)} %gain1_ref.1, bf16[3072,384]{1,0:T(8,128)(2,1)} %bitcast.19, bf16[3072,128]{1,0:T(8,128)(2,1)} %bitcast.21, bf16[3072,128]{1,0:T(8,128)(2,1)} %bitcast.22, bf16[384,3072]{1,0:T(8,128)(2,1)} %bitcast.20, ...), custom_call_target="tpu_custom_call" | custom-call | flops 22000001024 | bytes 26000000 | tf_op jit(solution)/shard_map/layer/pallas_call | solution.py:628
  129.2 1.6 %copy.16 = bf16[1,32,3072]{2,1,0:T(8,128)(2,1)} copy(bf16[1,32,3072]{2,1,0:T(8,128)(2,1)} %bitcast.15) | data formatting | bytes 393216

commit v3 on v2

--- a/solution.py
+++ b/solution.py
@@ -26,9 +26,14 @@
 
 OWN, Z, L, R, LZ, RZ, O, OZ = range(8)
 SLOTS = 8 * CAP
-PART_SLOTS = SLOTS // 2
+HALF_SLOTS = SLOTS // 2
 SPLIT = 2048
 SPLIT_BACK = 2048
+PROJ_CUT = 1664
+TOKENS_CUT = 640
+SPLIT_CUT = 1152
+BACK_CUT = 1152
+MOE_CUT = 640
 META = 16
 X_ROWS = SEQ + META
 
@@ -82,6 +87,10 @@
     def step(self, number):
         if number == 0:
             self.start("b_r", "b_l", "a_z", "a_r", "a_l", "b_z")
+        if number == "part 0":
+            self.start("a_z", "a_r", "a_l")
+        if number == "part 1":
+            self.start("b_r", "b_l", "b_z")
         if number == 1:
             self.arrive("b_r")
             self.start("lb_r", "lb_z")
@@ -112,15 +121,16 @@
         left, right, across = peers
         self.at = at
         self.relay_a, self.full_a, self.across_a, self.across_b, self.relay_b, self.full_b = buffers
+
+        def halved(ref, i, half):
+            count = ref.shape[1] // 2
+            return ref.at[i, pl.ds(half * count, count)]
+
         self.copies = {
             "oz_r": copy(at(OZ, 0, 0), self.relay_a.at[2], right),
             "oz_l": copy(at(OZ, 0, 1), self.relay_a.at[3], left),
             "o_r": copy(at(O, 0, 0), self.relay_a.at[0], right),
             "o_l": copy(at(O, 0, 1), self.relay_a.at[1], left),
-            "rz_r": copy(at(RZ, 0, None), self.full_a.at[2], right),
-            "lz_l": copy(at(LZ, 0, None), self.full_a.at[3], left),
-            "r_r": copy(at(R, 0, None), self.full_a.at[0], right),
-            "l_l": copy(at(L, 0, None), self.full_a.at[1], left),
             "z_z": copy(at(Z, 0, None), self.across_a, across),
             "b_own": copy(at(Z, 1, None), self.across_b.at[0], across),
             "b_left": copy(at(LZ, 1, None), self.across_b.at[1], across),
@@ -128,9 +138,14 @@
             "b_opp": copy(at(OZ, 1, None), self.across_b.at[3], across),
             "bo_r": copy(at(O, 1, 0), self.relay_b.at[0], right),
             "bo_l": copy(at(O, 1, 1), self.relay_b.at[1], left),
-            "br_r": copy(at(R, 1, None), self.full_b.at[0], right),
-            "bl_l": copy(at(L, 1, None), self.full_b.at[1], left),
         }
+        for half in (0, 1):
+            self.copies["rz%d" % half] = copy(at(RZ, 0, half), halved(self.full_a, 2, half), right)
+            self.copies["lz%d" % half] = copy(at(LZ, 0, half), halved(self.full_a, 3, half), left)
+            self.copies["r%d" % half] = copy(at(R, 0, half), halved(self.full_a, 0, half), right)
+            self.copies["l%d" % half] = copy(at(L, 0, half), halved(self.full_a, 1, half), left)
+            self.copies["br%d" % half] = copy(at(R, 1, half), halved(self.full_b, 0, half), right)
+            self.copies["bl%d" % half] = copy(at(L, 1, half), halved(self.full_b, 1, half), left)
 
     def start(self, *names):
         for name in names:
@@ -147,18 +162,28 @@
             total = total + term[...].astype(F32)
         ref[...] = total.astype(BF)
 
-    def early(self):
-        self.start("b_left", "b_right", "b_own")
+    def total(self, part, *terms):
+        result = self.at(OWN, part, None)[...].astype(F32)
+        for term in terms:
+            result = result + term.astype(F32)
+        return result
+
+    def near(self):
+        self.start("r1", "l0", "b_own")
+
+    def middle(self):
+        self.start("rz1", "lz0", "b_left")
+
+    def far(self):
+        self.start("oz_r", "oz_l", "b_opp", "o_r", "o_l", "b_right")
 
     def run(self):
-        self.start("oz_r", "oz_l", "b_opp", "o_r", "o_l")
-        yield
         self.arrive("oz_r")
         self.add(RZ, 0, 0, self.relay_a.at[2])
-        self.start("rz_r")
+        self.start("rz0")
         self.arrive("oz_l")
         self.add(LZ, 0, 1, self.relay_a.at[3])
-        self.start("lz_l")
+        self.start("lz1")
         yield
         self.arrive("b_opp")
         self.add(O, 1, None, self.across_b.at[3])
@@ -166,39 +191,34 @@
         yield
         self.arrive("o_r")
         self.add(R, 0, 0, self.relay_a.at[0])
-        self.start("r_r")
+        self.start("r0")
         self.arrive("o_l")
         self.add(L, 0, 1, self.relay_a.at[1])
-        self.start("l_l")
+        self.start("l1")
         yield
-        self.arrive("b_right", "b_left")
-        self.add(R, 1, None, self.across_b.at[2])
-        self.add(L, 1, None, self.across_b.at[1])
-        self.arrive("bo_r")
-        self.add(R, 1, 0, self.relay_b.at[0])
-        self.start("br_r")
-        self.arrive("bo_l")
-        self.add(L, 1, 1, self.relay_b.at[1])
-        self.start("bl_l")
-        yield
-        self.arrive("rz_r", "lz_l")
+        self.arrive("rz0", "rz1", "lz0", "lz1")
         self.add(Z, 0, None, self.full_a.at[2], self.full_a.at[3])
         self.start("z_z")
         yield
-        self.arrive("r_r", "l_l", "b_own", "br_r", "bl_l")
-        part_b = (
-            self.at(OWN, 1, None)[...].astype(F32)
-            + self.across_b[0].astype(F32)
-            + self.full_b[0].astype(F32)
-            + self.full_b[1].astype(F32)
-        )
-        part_a = (
-            self.at(OWN, 0, None)[...].astype(F32)
-            + self.full_a[0].astype(F32)
-            + self.full_a[1].astype(F32)
-        )
-        self.arrive("z_z")
-        self.sums = part_a + self.across_a[...].astype(F32), part_b
+        self.arrive("b_right")
+        self.add(R, 1, None, self.across_b.at[2])
+        self.start("br1")
+        self.arrive("b_left")
+        self.add(L, 1, None, self.across_b.at[1])
+        self.start("bl0")
+        yield
+        self.arrive("bo_r")
+        self.add(R, 1, 0, self.relay_b.at[0])
+        self.start("br0")
+        self.arrive("bo_l")
+        self.add(L, 1, 1, self.relay_b.at[1])
+        self.start("bl1")
+        yield
+        self.arrive("r0", "r1", "l0", "l1", "z_z")
+        self.sum_a = self.total(0, self.full_a[0], self.full_a[1], self.across_a[...])
+        yield
+        self.arrive("b_own", "br0", "br1", "bl0", "bl1")
+        self.sum_b = self.total(1, self.across_b[0], self.full_b[0], self.full_b[1])
 
     def finish(self):
         for one in self.copies.values():
@@ -225,10 +245,11 @@
 
 
 def layer(
-    x_ref, gain1_ref, wq_ref, wk_ref, wv_ref, wo_ref, gain2_ref, wg_ref, wu_ref, wd_ref, ids_ref, weights_ref,
-    cos_ref, sin_ref, out_ref,
+    x_ref, gain1_hbm, wq_ref, wk_ref, wv_ref, wo_ref, gain2_hbm, wg_ref, wu_ref, wd_ref, ids_hbm, weights_hbm,
+    cos_hbm, sin_hbm, out_ref,
+    ids_ref, weights_ref, gain1_ref, gain2_ref, cos_ref, sin_ref,
     wqkv, wo, wg, wu, wd, xs, acc, heads, mixed, proj, state, tables, combine, outgoing, tokens, wide_out, rows, act,
-    part, final, returned, wide_back, moe, handed,
+    part, final, returned, wide_back, moe, state_out, state_other, state_wide, meta_other,
     p_relay_a, p_full_a, p_across_a, p_across_b, p_relay_b, p_full_b,
     d_relay_a, d_full_a, d_across_a, d_across_b, d_relay_b, d_full_b,
     m_relay_a, m_full_a, m_across_a, m_across_b, m_relay_b, m_full_b,
@@ -259,18 +280,25 @@
         pl.semaphore_signal(barrier, inc=1, device_id=device, device_id_type=MESH)
     for dz, dy in hops:
         e_to, _, k_to = exchange(dz, dy)
-        pl.semaphore_signal(barrier, inc=1, device_id=(pipe, e_to, k_to), device_id_type=MESH)
+        for section in (pipe, 1 - pipe):
+            pl.semaphore_signal(barrier, inc=1, device_id=(section, e_to, k_to), device_id_type=MESH)
     pl.semaphore_signal(barrier, inc=1, device_id=other_core, device_id_type=MESH)
 
     loads = [
         pltpu.make_async_copy(source, target, load_sem.at[i])
         for i, (source, target) in enumerate(
             (
+                (ids_hbm, ids_ref),
+                (weights_hbm, weights_ref),
                 (x_ref, xs.at[0, pl.ds(0, SEQ)]),
+                (gain1_hbm, gain1_ref),
                 (wq_ref, wqkv.at[:, pl.ds(0, 384)]),
                 (wk_ref, wqkv.at[:, pl.ds(384, 128)]),
                 (wv_ref, wqkv.at[:, pl.ds(512, 128)]),
+                (cos_hbm, cos_ref),
+                (sin_hbm, sin_ref),
                 (wo_ref, wo),
+                (gain2_hbm, gain2_ref),
                 (wg_ref, wg),
                 (wu_ref, wu),
                 (wd_ref, wd),
@@ -280,6 +308,8 @@
     for one in loads:
         one.start()
 
+    for one in loads[:2]:
+        one.wait()
     xs[0, SEQ:X_ROWS, :] = jnp.zeros((META, COLS), BF)
     meta_row = lax.broadcasted_iota(jnp.int32, (META, TOK), 0)
     meta_rows = [ids_ref[0:1, :].astype(F32), ids_ref[1:2, :].astype(F32)]
@@ -288,8 +318,8 @@
     for i, row in enumerate(meta_rows):
         meta = jnp.where(meta_row == i, row, meta)
     xs[0, SEQ:X_ROWS, 0:TOK] = meta.astype(BF)
-    loads[0].wait()
-    pl.semaphore_wait(barrier, 4 + len(hops))
+    loads[2].wait()
+    pl.semaphore_wait(barrier, 4 + 2 * len(hops))
 
     used = [0]
 
@@ -323,7 +353,9 @@
         state[:, pl.ds(offset, COLS)] = xs[place, own_rows, :].astype(F32)
 
     features.step(0)
-    for one in loads[1:4]:
+    meta_copy = copy(xs.at[OWN, pl.ds(SEQ, META)], meta_other, other_core)
+    meta_copy.start()
+    for one in loads[3:7]:
         one.wait()
     project(OWN)
     features.step(1)
@@ -337,6 +369,8 @@
     for place in (O, OZ):
         project(place)
 
+    for one in loads[7:11]:
+        one.wait()
     factor = lax.rsqrt(sum(squares) * (1.0 / D) + epsilon)
     for i in range(5):
         block = acc[:, i * HD : (i + 1) * HD] * factor
@@ -353,7 +387,6 @@
         expo = jnp.exp(scores - jnp.max(scores, axis=1, keepdims=True))
         probs = (expo / jnp.sum(expo, axis=1, keepdims=True)).astype(BF)
         mixed[:, i * HD : (i + 1) * HD] = jnp.dot(probs, values, preferred_element_type=F32).astype(BF)
-    loads[4].wait()
 
     def out_columns(n, carry):
         columns = pl.ds(pl.multiple_of(n * 512, 512), 512)
@@ -362,68 +395,75 @@
 
     lax.fori_loop(0, D // 512, out_columns, 0)
 
-    def proj_at(place, part_no, half):
-        first = pl.multiple_of(index_of[place] * TOK + part_no * 16, 16)
-        columns = pl.ds(0, D) if half is None else pl.ds(half * (D // 2), D // 2)
-        return proj.at[pl.ds(first, 16), columns]
+    def cut_at(block_of, count, cut, width):
+        def at(place, part_no, half):
+            ref, first = block_of(place)
+            rows_here = pl.ds(first, count)
+            if half is not None:
+                rows_here = pl.ds(first + half * (count // 2), count // 2)
+            return ref.at[rows_here, pl.ds(0, cut) if part_no == 0 else pl.ds(cut, width - cut)]
+
+        return at
+
+    def proj_block(place):
+        return proj, pl.multiple_of(index_of[place] * TOK, TOK)
+
+    proj_at = cut_at(proj_block, TOK, PROJ_CUT, D)
 
     attention = Reduce(
         copy, proj_at, (p_relay_a, p_full_a, p_across_a, p_across_b, p_relay_b, p_full_b), peers
     )
-    attention.early()
+    attention.far()
+    attention.middle()
+    attention.near()
     running = attention.run()
-    next(running)
-
-    for place in range(8):
-        sent = xs[place, SEQ:X_ROWS, 0:TOK].astype(F32)
+
+    def routes(sent):
         first_route, second_route = placed(sent[0:1], sent[1:2])
-        tables[place] = (first_route + second_route).astype(BF)
         weight = first_route * (sent[2:3] + sent[3:4] + sent[4:5])
         weight = weight + second_route * (sent[5:6] + sent[6:7] + sent[7:8])
+        return first_route + second_route, weight
+
+    for place in range(8):
+        table, weight = routes(xs[place, SEQ:X_ROWS, 0:TOK].astype(F32))
+        tables[place] = table.astype(BF)
         high = weight.astype(BF)
         combine[0, place] = high
         combine[1, place] = (weight - high.astype(F32)).astype(BF)
 
-    def combined(place, outputs):
+    def combined(high, low, outputs):
         over_slots = (((0,), (0,)), ((), ()))
-        total = lax.dot_general(combine[0, place], outputs, over_slots, preferred_element_type=F32)
-        return total + lax.dot_general(combine[1, place], outputs, over_slots, preferred_element_type=F32)
+        total = lax.dot_general(high, outputs, over_slots, preferred_element_type=F32)
+        return total + lax.dot_general(low, outputs, over_slots, preferred_element_type=F32)
 
     for _ in running:
         pass
-    sum_a, sum_b = attention.sums
-    state[0:16, :] = (state[0:16, :] + sum_a).astype(BF).astype(F32)
-    state[16:32, :] = (state[16:32, :] + sum_b).astype(BF).astype(F32)
+    state[:, PROJ_CUT:] = (state[:, PROJ_CUT:] + attention.sum_b).astype(BF).astype(F32)
+    state[:, :PROJ_CUT] = (state[:, :PROJ_CUT] + attention.sum_a).astype(BF).astype(F32)
     state_now = state[...]
     factor2 = lax.rsqrt(jnp.mean(state_now * state_now, axis=1, keepdims=True) + epsilon)
     ffn_in = (state_now * factor2 * gain2_ref[...].astype(F32)).astype(BF)
 
     tokens[OWN] = ffn_in[:, SPLIT:]
 
-    def halves_at(ref, first_rows, rows_each, first_columns, width):
-        def at(place, part_no, half):
-            columns = pl.ds(first_columns, width)
-            if half is not None:
-                columns = pl.ds(first_columns + half * (width // 2), width // 2)
-            return ref.at[place, pl.ds(first_rows + part_no * rows_each, rows_each), columns]
-
-        return at
-
-    spread = Gather(copy, halves_at(tokens, 0, 16, 0, D - SPLIT), peers)
+    spread = Gather(copy, cut_at(lambda place: (tokens.at[place], 0), TOK, TOKENS_CUT, D - SPLIT), peers)
     spread.step(0)
 
     outgoing[...] = jnp.dot(tables[OWN], ffn_in[:, :SPLIT], preferred_element_type=F32).astype(BF)
     sends = []
-    for dz, dy in hops:
-        e_to, _, k_to = exchange(dz, dy)
-        sends.append(
-            copy(
-                outgoing.at[pl.ds(pl.multiple_of(e_to * CAP, CAP), CAP)],
-                rows.at[OWN, pl.ds(pl.multiple_of(dz * PART_SLOTS + y * CAP, CAP), CAP), pl.ds(0, SPLIT)],
-                (pipe, e_to, k_to),
+    for columns in (pl.ds(SPLIT_CUT, SPLIT - SPLIT_CUT), pl.ds(0, SPLIT_CUT)):
+        copies = []
+        for dz, dy in hops:
+            e_to, _, k_to = exchange(dz, dy)
+            copies.append(
+                copy(
+                    outgoing.at[pl.ds(pl.multiple_of(e_to * CAP, CAP), CAP), columns],
+                    rows.at[OWN, pl.ds(pl.multiple_of(dz * HALF_SLOTS + y * CAP, CAP), CAP), columns],
+                    (pipe, e_to, k_to),
+                )
             )
-        )
-        sends[-1].start()
+            copies[-1].start()
+        sends.append(copies)
     own_slots = pl.ds(pl.multiple_of(exp * CAP, CAP), CAP)
     own_block = pl.ds(pl.multiple_of(y * CAP, CAP), CAP)
     rows[OWN, own_block, 0:SPLIT] = outgoing[own_slots, :]
@@ -442,7 +482,7 @@
                     wide_out.at[e_to, pl.ds(2 * group, 2)],
                     rows.at[
                         pl.ds(2 * group, 2),
-                        pl.ds(pl.multiple_of(dz * PART_SLOTS + y * CAP, CAP), CAP),
+                        pl.ds(pl.multiple_of(dz * HALF_SLOTS + y * CAP, CAP), CAP),
                         pl.ds(SPLIT, D - SPLIT),
                     ],
                     (pipe, e_to, k_to),
@@ -453,26 +493,33 @@
             rows[place, own_block, SPLIT:] = wide_out[exp, place]
         wide_sends.append(copies)
 
+    dispatch = Gather(copy, cut_at(lambda place: (rows.at[place], 0), SLOTS, SPLIT_CUT, SPLIT), peers)
+    shares = Reduce(
+        copy,
+        cut_at(lambda place: (part.at[place], 0), SLOTS, BACK_CUT, SPLIT_BACK),
+        (d_relay_a, d_full_a, d_across_a, d_across_b, d_relay_b, d_full_b),
+        peers,
+    )
+    narrow = shares.run()
+
     spread.step(1)
     widen(0)
     spread.step(2)
+    for one in sends[0]:
+        one.wait_recv()
+    dispatch.step("part 1")
     widen(1)
     spread.step(3)
     widen(2)
+    for one in sends[1]:
+        one.wait_recv()
+    dispatch.step("part 0")
     spread.step(4)
     widen(3)
-
-    dispatch = Gather(copy, lambda place, part_no, half: rows.at[
-        place,
-        pl.ds(part_no * PART_SLOTS + (half or 0) * (PART_SLOTS // 2), PART_SLOTS // (1 if half is None else 2)),
-        pl.ds(0, SPLIT),
-    ], peers)
-    shares = Reduce(
-        copy,
-        halves_at(part, 0, PART_SLOTS, 0, SPLIT_BACK),
-        (d_relay_a, d_full_a, d_across_a, d_across_b, d_relay_b, d_full_b),
-        peers,
-    )
+    state_out[...] = state[:, :SPLIT_BACK].astype(BF)
+    state_copy = copy(state_out, state_other, other_core)
+    state_copy.start()
+
     wide_backs = []
     for group in range(4):
         copies = []
@@ -482,7 +529,7 @@
                 copy(
                     part.at[
                         pl.ds(2 * group, 2),
-                        pl.ds(pl.multiple_of(dz * PART_SLOTS + y_to * CAP, CAP), CAP),
+                        pl.ds(pl.multiple_of(dz * HALF_SLOTS + y_to * CAP, CAP), CAP),
                         pl.ds(SPLIT_BACK, D - SPLIT_BACK),
                     ],
                     wide_back.at[pl.ds(2 * group, 2), own_slots],
@@ -491,10 +538,7 @@
             )
         wide_backs.append(copies)
 
-    for one in sends:
-        one.wait_recv()
-    dispatch.step(0)
-    for one in loads[5:]:
+    for one in loads[11:]:
         one.wait()
 
     def expert(group, carry):
@@ -502,31 +546,34 @@
 
             @pl.when(group == number)
             def _(number=number):
+                if number == 3:
+                    shares.middle()
                 dispatch.step(number + 1)
+                if number == 2:
+                    shares.near()
                 for one in wide_sends[number]:
                     one.wait_recv()
-                if number == 3:
-                    shares.early()
 
         places = pl.ds(group * 2, 2)
 
-        def hidden(n, inner):
-            columns = pl.ds(pl.multiple_of(n * 512, 512), 512)
-            block = rows[places].reshape(2 * SLOTS, D)
-            gate = jnp.dot(block, wg[:, columns], preferred_element_type=F32)
-            upper = jnp.dot(block, wu[:, columns], preferred_element_type=F32)
-            act[:, columns] = (gate / (1.0 + jnp.exp(-gate)) * upper).astype(BF)
+        block = rows[places].reshape(2 * SLOTS, D)
+        gate = jnp.dot(block, wg[...], preferred_element_type=F32)
+        upper = jnp.dot(block, wu[...], preferred_element_type=F32)
+        act[...] = (gate / (1.0 + jnp.exp(-gate)) * upper).astype(BF)
+
+        def down(n, inner):
+            columns = pl.ds(pl.multiple_of(n * 1024, 1024), 1024)
+            block = jnp.dot(act[...], wd[:, columns], preferred_element_type=F32).astype(BF)
+            part[places, :, columns] = block.reshape(2, SLOTS, 1024)
             return inner
 
-        lax.fori_loop(0, HID // 512, hidden, 0)
-
-        def down(n, inner):
-            columns = pl.ds(pl.multiple_of(n * 512, 512), 512)
-            block = jnp.dot(act[...], wd[:, columns], preferred_element_type=F32).astype(BF)
-            part[places, :, columns] = block.reshape(2, SLOTS, 512)
-            return inner
-
-        lax.fori_loop(0, D // 512, down, 0)
+        lax.fori_loop(0, -(-SPLIT_BACK // 1024), down, 0)
+
+        @pl.when(group == 3)
+        def _():
+            shares.far()
+
+        lax.fori_loop(-(-SPLIT_BACK // 1024), D // 1024, down, 0)
         for number in range(4):
 
             @pl.when(group == number)
@@ -542,69 +589,87 @@
 
     sums = Reduce(
         copy,
-        halves_at(moe, 0, 16, 0, D - SPLIT_BACK),
+        cut_at(lambda place: (moe.at[place], 0), TOK, MOE_CUT, D - SPLIT_BACK),
         (m_relay_a, m_full_a, m_across_a, m_across_b, m_relay_b, m_full_b),
         peers,
     )
-    narrow, wide = shares.run(), sums.run()
-    for _ in range(4):
+    wide = sums.run()
+    for _ in range(3):
         next(narrow)
     for group in range(4):
         for one in wide_backs[group]:
             one.wait_recv()
         for place in (2 * group, 2 * group + 1):
-            moe[place] = combined(place, wide_back[place]).astype(BF)
-    sums.early()
-    next(wide)
-    next(narrow)
-    next(wide)
-    next(wide)
+            moe[place] = combined(combine[0, place], combine[1, place], wide_back[place]).astype(BF)
+    sums.far()
+    sums.middle()
+    sums.near()
     next(narrow)
     for _ in range(3):
         next(wide)
+    next(narrow)
+    next(wide)
+    next(narrow)
+    for _ in range(2):
+        next(wide)
+
+    backs = []
+
+    def send_back(columns):
+        copies = []
+        for dz, dy in hops + [(0, 0)]:
+            e_to, y_to, k_to = exchange(dz, dy)
+            copies.append(
+                copy(
+                    final.at[pl.ds(pl.multiple_of(dz * HALF_SLOTS + y_to * CAP, CAP), CAP), columns],
+                    returned.at[own_slots, columns],
+                    (1 - pipe, e_to, k_to),
+                )
+            )
+            copies[-1].start()
+        backs.append(copies)
+
+    meta_copy.wait_recv()
+    _, weight = routes(meta_other[:, 0:TOK].astype(F32))
+    high = weight.astype(BF)
+    low = (weight - high.astype(F32)).astype(BF)
+    next(narrow)
+    final[:, :BACK_CUT] = shares.sum_a.astype(BF)
+    send_back(pl.ds(0, BACK_CUT))
+    next(wide)
     for _ in narrow:
         pass
-    sum_a, sum_b = shares.sums
-    final[0:PART_SLOTS, :] = sum_a.astype(BF)
-    final[PART_SLOTS:, :] = sum_b.astype(BF)
-
-    backs = []
-    for dz, dy in hops:
-        e_to, y_to, k_to = exchange(dz, dy)
-        backs.append(
-            copy(
-                final.at[pl.ds(pl.multiple_of(dz * PART_SLOTS + y_to * CAP, CAP), CAP)],
-                returned.at[own_slots],
-                (pipe, e_to, k_to),
-            )
-        )
-        backs[-1].start()
-    returned[own_slots, :] = final[own_block, :]
+    final[:, BACK_CUT:] = shares.sum_b.astype(BF)
+    send_back(pl.ds(BACK_CUT, SPLIT_BACK - BACK_CUT))
     for _ in wide:
         pass
-    sum_a, sum_b = sums.sums
-    handed[0:16, SPLIT_BACK:] = (state[0:16, SPLIT_BACK:] + sum_a).astype(BF)
-    handed[16:32, SPLIT_BACK:] = (state[16:32, SPLIT_BACK:] + sum_b).astype(BF)
-    for one in backs:
-        one.wait_recv()
-    handed[:, :SPLIT_BACK] = (state[:, :SPLIT_BACK] + combined(OWN, returned[...])).astype(BF)
-    handing = copy(handed, out_ref, other_core)
-    handing.start()
+    border = SPLIT_BACK + MOE_CUT
+    state_wide[:, MOE_CUT:] = (state[:, border:] + sums.sum_b).astype(BF)
+    state_wide[:, :MOE_CUT] = (state[:, SPLIT_BACK:border] + sums.sum_a).astype(BF)
+    wide_copy = copy(state_wide, out_ref.at[:, pl.ds(SPLIT_BACK, D - SPLIT_BACK)], other_core)
+    wide_copy.start()
+    state_copy.wait_recv()
+    for copies, columns in zip(backs, (slice(0, BACK_CUT), slice(BACK_CUT, SPLIT_BACK))):
+        for one in copies:
+            one.wait_recv()
+        total = state_other[:, columns].astype(F32) + combined(high, low, returned[:, columns])
+        out_ref[:, columns] = total.astype(BF)
     for one in (features, attention, spread, dispatch, shares, sums):
         one.finish()
-    for one in sum(wide_sends + wide_backs, sends + backs):
+    for one in sum(sends + wide_sends + wide_backs + backs, [meta_copy, state_copy]):
         one.wait_send()
-    handing.wait()
-
-
-def buffers(part_rows, width):
+    wide_copy.wait()
+
+
+def buffers(rows, cut, width):
+    rest = width - cut
     return [
-        pltpu.VMEM((4, part_rows, width // 2), BF),
-        pltpu.VMEM((4, part_rows, width), BF),
-        pltpu.VMEM((part_rows, width), BF),
-        pltpu.VMEM((4, part_rows, width), BF),
-        pltpu.VMEM((2, part_rows, width // 2), BF),
-        pltpu.VMEM((2, part_rows, width), BF),
+        pltpu.VMEM((4, rows // 2, cut), BF),
+        pltpu.VMEM((4, rows, cut), BF),
+        pltpu.VMEM((rows, cut), BF),
+        pltpu.VMEM((4, rows, rest), BF),
+        pltpu.VMEM((2, rows // 2, rest), BF),
+        pltpu.VMEM((2, rows, rest), BF),
     ]
 
 
@@ -624,13 +689,18 @@
 ):
     cosine, sine = rope_tables()
     anywhere = pl.BlockSpec(memory_space=pl.ANY)
-    vmem = pl.BlockSpec(memory_space=pltpu.VMEM)
     handed = pl.pallas_call(
         layer,
         out_shape=jax.ShapeDtypeStruct((TOK, D), BF),
-        in_specs=[anywhere, vmem] + [anywhere] * 4 + [vmem] + [anywhere] * 3 + [vmem] * 4,
-        out_specs=anywhere,
+        in_specs=[anywhere] * 14,
+        out_specs=pl.BlockSpec(memory_space=pltpu.VMEM),
         scratch_shapes=[
+            pltpu.VMEM((2, TOK), jnp.int32),
+            pltpu.VMEM((2, TOK), F32),
+            pltpu.VMEM((1, D), BF),
+            pltpu.VMEM((1, D), BF),
+            pltpu.VMEM((SEQ, HD), F32),
+            pltpu.VMEM((SEQ, HD), F32),
             pltpu.VMEM((D, QKV), BF),
             pltpu.VMEM((384, D), BF),
             pltpu.VMEM((D, HID), BF),
@@ -654,13 +724,16 @@
             pltpu.VMEM((SLOTS, SPLIT_BACK), BF),
             pltpu.VMEM((8, SLOTS, D - SPLIT_BACK), BF),
             pltpu.VMEM((8, TOK, D - SPLIT_BACK), BF),
-            pltpu.VMEM((TOK, D), BF),
-            *buffers(16, D),
-            *buffers(PART_SLOTS, SPLIT_BACK),
-            *buffers(16, D - SPLIT_BACK),
-            pltpu.SemaphoreType.DMA((8,)),
-            pltpu.SemaphoreType.DMA((174,)),
-            pltpu.SemaphoreType.DMA((174,)),
+            pltpu.VMEM((TOK, SPLIT_BACK), BF),
+            pltpu.VMEM((TOK, SPLIT_BACK), BF),
+            pltpu.VMEM((TOK, D - SPLIT_BACK), BF),
+            pltpu.VMEM((META, COLS), BF),
+            *buffers(TOK, PROJ_CUT, D),
+            *buffers(SLOTS, BACK_CUT, SPLIT_BACK),
+            *buffers(TOK, MOE_CUT, D - SPLIT_BACK),
+            pltpu.SemaphoreType.DMA((14,)),
+            pltpu.SemaphoreType.DMA((216,)),
+            pltpu.SemaphoreType.DMA((216,)),
         ],
         compiler_params=pltpu.CompilerParams(
             collective_id=0, has_side_effects=True, vmem_limit_bytes=60 * 2**20

time: 131 us -> 119 us (0.908)
  Pallas kernels: 129 us -> 117 us
    pallas_call x1, Pallas kernels: 129 us -> 117 us  [on_device(): pl.pallas_call(layer, out_shape=jax.ShapeDtypeStruct((TOK, D), BF), in_sp...]
where the time goes in v3:
time: 119 us
  Pallas kernels  117 us (98%)
  local copies, waits for them, and re-layouts  1.62 us (1%)
    pallas_call x1, Pallas kernels, on_device(): pl.pallas_call(layer, out_shape=jax.ShapeDtypeStruct((TOK, D), BF), in_sp...  117 us

profile of v3, /device:TPU:1, one launch (start us, length us, event | category | flops | bytes accessed | tf_op | source)
XLA Modules:
  0.0 118.6 jit_solution(6808641937298780692)
XLA Ops:
  0.0 117.0 %layer.1 = bf16[32,3072]{1,0:T(8,128)(2,1)} custom-call(bf16[256,384]{1,0:T(8,128)(2,1)} %bitcast.23, bf16[1,3072]{1,0:T(2,128)(2,1)} %gain1_hbm.1, bf16[3072,384]{1,0:T(8,128)(2,1)} %bitcast.19, bf16[3072,128]{1,0:T(8,128)(2,1)} %bitcast.21, bf16[3072,128]{1,0:T(8,128)(2,1)} %bitcast.22, bf16[384,3072]{1,0:T(8,128)(2,1)} %bitcast.20, ...), custom_call_target="tpu_custom_call" | custom-call | flops 22000001024 | bytes 26000000 | tf_op jit(solution)/shard_map/layer/pallas_call | solution.py:692
  117.0 1.6 %copy.16 = bf16[1,32,3072]{2,1,0:T(8,128)(2,1)} copy(bf16[1,32,3072]{2,1,0:T(8,128)(2,1)} %bitcast.15) | data formatting | bytes 393216

commit v4 on v3

--- a/solution.py
+++ b/solution.py
@@ -594,25 +594,6 @@
         peers,
     )
     wide = sums.run()
-    for _ in range(3):
-        next(narrow)
-    for group in range(4):
-        for one in wide_backs[group]:
-            one.wait_recv()
-        for place in (2 * group, 2 * group + 1):
-            moe[place] = combined(combine[0, place], combine[1, place], wide_back[place]).astype(BF)
-    sums.far()
-    sums.middle()
-    sums.near()
-    next(narrow)
-    for _ in range(3):
-        next(wide)
-    next(narrow)
-    next(wide)
-    next(narrow)
-    for _ in range(2):
-        next(wide)
-
     backs = []
 
     def send_back(columns):
@@ -629,14 +610,29 @@
             copies[-1].start()
         backs.append(copies)
 
+    for _ in range(3):
+        next(narrow)
+    for group in range(4):
+        for one in wide_backs[group]:
+            one.wait_recv()
+        for place in (2 * group, 2 * group + 1):
+            moe[place] = combined(combine[0, place], combine[1, place], wide_back[place]).astype(BF)
+    sums.far()
+    sums.middle()
+    sums.near()
+    for _ in range(3):
+        next(narrow)
     meta_copy.wait_recv()
     _, weight = routes(meta_other[:, 0:TOK].astype(F32))
     high = weight.astype(BF)
     low = (weight - high.astype(F32)).astype(BF)
+    for _ in range(3):
+        next(wide)
     next(narrow)
     final[:, :BACK_CUT] = shares.sum_a.astype(BF)
     send_back(pl.ds(0, BACK_CUT))
-    next(wide)
+    for _ in range(3):
+        next(wide)
     for _ in narrow:
         pass
     final[:, BACK_CUT:] = shares.sum_b.astype(BF)

time: 119 us -> 115 us (0.966)
  Pallas kernels: 117 us -> 113 us
    pallas_call x1, Pallas kernels: 117 us -> 113 us  [on_device(): pl.pallas_call(layer, out_shape=jax.ShapeDtypeStruct((TOK, D), BF), in_sp...]
where the time goes in v4:
time: 115 us; the launch traced here: 114 us
  Pallas kernels  113 us (98%)
  local copies, waits for them, and re-layouts  1.62 us (1%)
    pallas_call x1, Pallas kernels, on_device(): pl.pallas_call(layer, out_shape=jax.ShapeDtypeStruct((TOK, D), BF), in_sp...  113 us

profile of v4, /device:TPU:1, one launch (start us, length us, event | category | flops | bytes accessed | tf_op | source)
XLA Modules:
  0.0 114.4 jit_solution(13470152267209723395)
XLA Ops:
  0.0 112.8 %layer.1 = bf16[32,3072]{1,0:T(8,128)(2,1)} custom-call(bf16[256,384]{1,0:T(8,128)(2,1)} %bitcast.23, bf16[1,3072]{1,0:T(2,128)(2,1)} %gain1_hbm.1, bf16[3072,384]{1,0:T(8,128)(2,1)} %bitcast.19, bf16[3072,128]{1,0:T(8,128)(2,1)} %bitcast.21, bf16[3072,128]{1,0:T(8,128)(2,1)} %bitcast.22, bf16[384,3072]{1,0:T(8,128)(2,1)} %bitcast.20, ...), custom_call_target="tpu_custom_call" | custom-call | flops 22000001024 | bytes 26000000 | tf_op jit(solution)/shard_map/layer/pallas_call | solution.py:688
  112.8 1.6 %copy.16 = bf16[1,32,3072]{2,1,0:T(8,128)(2,1)} copy(bf16[1,32,3072]{2,1,0:T(8,128)(2,1)} %bitcast.15) | data formatting | bytes 393216

commit v5 on v4

--- a/solution.py
+++ b/solution.py
@@ -32,7 +32,7 @@
 PROJ_CUT = 1664
 TOKENS_CUT = 640
 SPLIT_CUT = 1152
-BACK_CUT = 1152
+BACK_CUT = 1024
 MOE_CUT = 640
 META = 16
 X_ROWS = SEQ + META
@@ -174,8 +174,15 @@
     def middle(self):
         self.start("rz1", "lz0", "b_left")
 
+    def far_along_x(self):
+        self.start("oz_r", "oz_l", "o_r", "o_l")
+
+    def far_along_z(self):
+        self.start("b_opp", "b_right")
+
     def far(self):
-        self.start("oz_r", "oz_l", "b_opp", "o_r", "o_l", "b_right")
+        self.far_along_z()
+        self.far_along_x()
 
     def run(self):
         self.arrive("oz_r")
@@ -393,8 +400,6 @@
         proj[:, columns] = jnp.dot(mixed[...], wo[:, columns], preferred_element_type=F32).astype(BF)
         return carry
 
-    lax.fori_loop(0, D // 512, out_columns, 0)
-
     def cut_at(block_of, count, cut, width):
         def at(place, part_no, half):
             ref, first = block_of(place)
@@ -413,7 +418,10 @@
     attention = Reduce(
         copy, proj_at, (p_relay_a, p_full_a, p_across_a, p_across_b, p_relay_b, p_full_b), peers
     )
-    attention.far()
+    lax.fori_loop(0, -(-PROJ_CUT // 512), out_columns, 0)
+    attention.far_along_x()
+    lax.fori_loop(-(-PROJ_CUT // 512), D // 512, out_columns, 0)
+    attention.far_along_z()
     attention.middle()
     attention.near()
     running = attention.run()
@@ -424,18 +432,23 @@
         weight = weight + second_route * (sent[5:6] + sent[6:7] + sent[7:8])
         return first_route + second_route, weight
 
-    for place in range(8):
-        table, weight = routes(xs[place, SEQ:X_ROWS, 0:TOK].astype(F32))
-        tables[place] = table.astype(BF)
-        high = weight.astype(BF)
-        combine[0, place] = high
-        combine[1, place] = (weight - high.astype(F32)).astype(BF)
+    def place_tokens(first, last):
+        for place in range(first, last):
+            table, _ = routes(xs[place, SEQ:X_ROWS, 0:TOK].astype(F32))
+            tables[place] = table.astype(BF)
+
+    place_tokens(0, 2)
 
     def combined(high, low, outputs):
         over_slots = (((0,), (0,)), ((), ()))
         total = lax.dot_general(high, outputs, over_slots, preferred_element_type=F32)
         return total + lax.dot_general(low, outputs, over_slots, preferred_element_type=F32)
 
+    next(running)
+    place_tokens(2, 4)
+    next(running)
+    next(running)
+    place_tokens(4, 8)
     for _ in running:
         pass
     state[:, PROJ_CUT:] = (state[:, PROJ_CUT:] + attention.sum_b).astype(BF).astype(F32)
@@ -538,8 +551,16 @@
             )
         wide_backs.append(copies)
 
+    for place in range(8):
+        _, weight = routes(xs[place, SEQ:X_ROWS, 0:TOK].astype(F32))
+        high = weight.astype(BF)
+        combine[0, place] = high
+        combine[1, place] = (weight - high.astype(F32)).astype(BF)
     for one in loads[11:]:
         one.wait()
+    for one in (features, attention):
+        one.finish()
+    meta_copy.wait_send()
 
     def expert(group, carry):
         for number in range(4):
@@ -567,13 +588,20 @@
             part[places, :, columns] = block.reshape(2, SLOTS, 1024)
             return inner
 
-        lax.fori_loop(0, -(-SPLIT_BACK // 1024), down, 0)
+        steps = (0, -(-BACK_CUT // 1024), -(-SPLIT_BACK // 1024), D // 1024)
+        lax.fori_loop(steps[0], steps[1], down, 0)
 
         @pl.when(group == 3)
         def _():
-            shares.far()
-
-        lax.fori_loop(-(-SPLIT_BACK // 1024), D // 1024, down, 0)
+            shares.far_along_x()
+
+        lax.fori_loop(steps[1], steps[2], down, 0)
+
+        @pl.when(group == 3)
+        def _():
+            shares.far_along_z()
+
+        lax.fori_loop(steps[2], steps[3], down, 0)
         for number in range(4):
 
             @pl.when(group == number)
@@ -626,6 +654,10 @@
     _, weight = routes(meta_other[:, 0:TOK].astype(F32))
     high = weight.astype(BF)
     low = (weight - high.astype(F32)).astype(BF)
+    for one in (spread, dispatch):
+        one.finish()
+    for one in sum(sends + wide_sends, [state_copy]):
+        one.wait_send()
     for _ in range(3):
         next(wide)
     next(narrow)
@@ -637,6 +669,9 @@
         pass
     final[:, BACK_CUT:] = shares.sum_b.astype(BF)
     send_back(pl.ds(BACK_CUT, SPLIT_BACK - BACK_CUT))
+    shares.finish()
+    for one in sum(wide_backs, []):
+        one.wait_send()
     for _ in wide:
         pass
     border = SPLIT_BACK + MOE_CUT
@@ -644,15 +679,14 @@
     state_wide[:, :MOE_CUT] = (state[:, SPLIT_BACK:border] + sums.sum_a).astype(BF)
     wide_copy = copy(state_wide, out_ref.at[:, pl.ds(SPLIT_BACK, D - SPLIT_BACK)], other_core)
     wide_copy.start()
+    sums.finish()
     state_copy.wait_recv()
     for copies, columns in zip(backs, (slice(0, BACK_CUT), slice(BACK_CUT, SPLIT_BACK))):
         for one in copies:
             one.wait_recv()
         total = state_other[:, columns].astype(F32) + combined(high, low, returned[:, columns])
         out_ref[:, columns] = total.astype(BF)
-    for one in (features, attention, spread, dispatch, shares, sums):
-        one.finish()
-    for one in sum(sends + wide_sends + wide_backs + backs, [meta_copy, state_copy]):
+    for one in sum(backs, []):
         one.wait_send()
     wide_copy.wait()
 

time: 115 us -> 113 us (0.983)
  Pallas kernels: 113 us -> 111 us
    pallas_call x1, Pallas kernels: 113 us -> 111 us  [on_device(): pl.pallas_call(layer, out_shape=jax.ShapeDtypeStruct((TOK, D), BF), in_sp...]
where the time goes in v5:
time: 113 us
  Pallas kernels  111 us (98%)
  local copies, waits for them, and re-layouts  1.62 us (1%)
    pallas_call x1, Pallas kernels, on_device(): pl.pallas_call(layer, out_shape=jax.ShapeDtypeStruct((TOK, D), BF), in_sp...  111 us

profile of v5, /device:TPU:1, one launch (start us, length us, event | category | flops | bytes accessed | tf_op | source)
XLA Modules:
  0.0 112.9 jit_solution(1858313732705809144)
XLA Ops:
  0.0 111.3 %layer.1 = bf16[32,3072]{1,0:T(8,128)(2,1)} custom-call(bf16[256,384]{1,0:T(8,128)(2,1)} %bitcast.23, bf16[1,3072]{1,0:T(2,128)(2,1)} %gain1_hbm.1, bf16[3072,384]{1,0:T(8,128)(2,1)} %bitcast.19, bf16[3072,128]{1,0:T(8,128)(2,1)} %bitcast.21, bf16[3072,128]{1,0:T(8,128)(2,1)} %bitcast.22, bf16[384,3072]{1,0:T(8,128)(2,1)} %bitcast.20, ...), custom_call_target="tpu_custom_call" | custom-call | flops 22000001024 | bytes 26000000 | tf_op jit(solution)/shard_map/layer/pallas_call | solution.py:722
  111.3 1.6 %copy.16 = bf16[1,32,3072]{2,1,0:T(8,128)(2,1)} copy(bf16[1,32,3072]{2,1,0:T(8,128)(2,1)} %bitcast.15) | data formatting | bytes 393216
